TPU v7x, 128 devices: a whole 4x4x4 slice. The times are simulated.
128 devices in a mesh: dp: 4 (over x), shard: 32 (over z, y, core).
Axes of the slice: x: 4, y: 4, z: 4, core: 2. Of those that a mesh axis runs over, the one named last changes fastest.
Arguments:
- tokens: bfloat16 [65536, 1024], P(('dp', 'shard')), may hold values from -6 to 6
- cotangent: bfloat16 [65536, 1024], P(('dp', 'shard')), may hold values from -6 to 6
- lengths: int32 [128, 4], P(('dp', 'shard')), may hold values from 1 to 256, 512 in all within a row
- levels: int32 [128, 4], P(('dp', 'shard')), may hold values from 0 to 7
- level_scale: float32 [8], replicated, may hold values from 0.25 to 4
- norm_gain: float32 [1024], replicated, may hold values from 0.25 to 1.75
- q_gain: float32 [128], replicated, may hold values from 0.5 to 3
- k_gain: float32 [128], replicated, may hold values from 0.5 to 3
- w_query: bfloat16 [1024, 2048], P('shard'), may hold values from -0.1875 to 0.1875
- w_key: bfloat16 [1024, 1024], P('shard'), may hold values from -0.1875 to 0.1875
- w_value: bfloat16 [1024, 1024], P('shard'), may hold values from -0.1875 to 0.1875
- w_output: bfloat16 [2048, 1024], P('shard'), may hold values from -0.125 to 0.125
Outputs:
- grad_tokens: bfloat16 [65536, 1024], P(('dp', 'shard'))
- grad_norm_gain: float32 [1024], replicated
- grad_q_gain: float32 [128], replicated
- grad_k_gain: float32 [128], replicated
- grad_w_query: float32 [1024, 2048], P('shard')
- grad_w_key: float32 [1024, 1024], P('shard')
- grad_w_value: float32 [1024, 1024], P('shard')
- grad_w_output: float32 [2048, 1024], P('shard')
Inputs may be any that keep to these rules, and one draw needn't show every extreme that they name: `lengths`: each row's 4 entries sum to 512; the last entry of a row counts padding tokens; every row has an entry equal to 256.
All inputs are finite; a program needn't handle non-finite values.
Results may differ from a plain program's by a relative error of at most 0.03.
Values may be sent and summed in bfloat16 or wider, within the bound.
No kernel may reach another device: no remote copies, remote signals or barrier semaphores. Data moves between devices by JAX's collectives and lax.ppermute only.
A program may use at most 128 MiB of HBM per device.

v0:
```python
import math

import jax
import jax.numpy as jnp
from jax import lax
from jax.sharding import PartitionSpec as P

norm_eps = 1e-06
rope_theta = 1000000.0


def row_layout(lengths, levels, level_scale, rows_total):
    slot_ends = jnp.cumsum(lengths)
    slot_starts = slot_ends - lengths
    places = jnp.arange(rows_total, dtype=jnp.int32)
    owner = jnp.sum((places[:, None] >= slot_ends[None, :]).astype(jnp.int32), axis=1)
    slot_ids = jnp.arange(lengths.shape[0], dtype=jnp.int32)
    member = owner[:, None] == slot_ids[None, :]
    positions = places - jnp.sum(jnp.where(member, slot_starts[None, :], 0), axis=1)
    level_ids = jnp.arange(level_scale.shape[0], dtype=jnp.int32)
    level_hit = levels[:, None] == level_ids[None, :]
    slot_weight = jnp.sum(jnp.where(level_hit, level_scale[None, :], jnp.float32(0.0)), axis=1)
    slot_weight = jnp.where(slot_ids < lengths.shape[0] - 1, slot_weight, jnp.float32(0.0))
    token_weight = jnp.sum(jnp.where(member, slot_weight[None, :], jnp.float32(0.0)), axis=1)
    return (owner, positions, token_weight)


def head_norm(heads_in, gains):
    factor = lax.rsqrt(jnp.mean(heads_in * heads_in, axis=-1, keepdims=True) + norm_eps)
    return heads_in * factor * gains


def rotate(heads_in, positions):
    head_dim = heads_in.shape[-1]
    half_dim = head_dim // 2
    freqs = rope_theta ** (-jnp.arange(half_dim, dtype=jnp.float32) * 2.0 / head_dim)
    angles = positions.astype(jnp.float32)[:, None] * freqs[None, :]
    cosine = jnp.cos(angles)
    sines = jnp.sin(angles)
    cosine = jnp.concatenate([cosine, cosine], axis=-1)[:, None, :]
    sines = jnp.concatenate([sines, sines], axis=-1)[:, None, :]
    turned = jnp.concatenate([-heads_in[..., half_dim:], heads_in[..., :half_dim]], axis=-1)
    return heads_in * cosine + turned * sines


def layer_branch(
    tokens_in, norm_gain, q_gain, k_gain, w_query, w_key, w_value, w_output, owner, positions
):
    rows_total = tokens_in.shape[0]
    head_dim = q_gain.shape[0]
    query_heads = w_query.shape[1] // head_dim
    key_heads = w_key.shape[1] // head_dim
    group_size = query_heads // key_heads
    widened = tokens_in.astype(jnp.float32)
    inverse = lax.rsqrt(jnp.mean(widened * widened, axis=-1, keepdims=True) + norm_eps)
    normed = (widened * inverse * norm_gain).astype(jnp.bfloat16)
    queries = jnp.dot(normed, w_query, preferred_element_type=jnp.float32).reshape(
        rows_total, query_heads, head_dim
    )
    keys_all = jnp.dot(normed, w_key, preferred_element_type=jnp.float32).reshape(
        rows_total, key_heads, head_dim
    )
    values_all = jnp.dot(normed, w_value, preferred_element_type=jnp.float32).astype(jnp.bfloat16)
    values_all = values_all.reshape(rows_total, key_heads, head_dim)
    queries = rotate(head_norm(queries, q_gain), positions).astype(jnp.bfloat16)
    keys_all = rotate(head_norm(keys_all, k_gain), positions).astype(jnp.bfloat16)
    grouped = queries.reshape(rows_total, key_heads, group_size, head_dim)
    scores = jnp.einsum("tkgd,skd->kgts", grouped, keys_all, preferred_element_type=jnp.float32)
    scores = scores * (1.0 / math.sqrt(head_dim))
    places = jnp.arange(rows_total, dtype=jnp.int32)
    allowed = (owner[:, None] == owner[None, :]) & (places[None, :] <= places[:, None])
    scores = jnp.where(allowed, scores, jnp.float32(-1e30))
    highest = lax.stop_gradient(jnp.max(scores, axis=-1, keepdims=True))
    raised = jnp.exp(scores - highest)
    probs = (raised / jnp.sum(raised, axis=-1, keepdims=True)).astype(jnp.bfloat16)
    mixed = jnp.einsum("kgts,skd->tkgd", probs, values_all, preferred_element_type=jnp.float32)
    mixed = mixed.astype(jnp.bfloat16).reshape(rows_total, query_heads * head_dim)
    return widened + jnp.dot(mixed, w_output, preferred_element_type=jnp.float32)


def body(
    tokens,
    cotangent,
    lengths,
    levels,
    level_scale,
    norm_gain,
    q_gain,
    k_gain,
    w_query,
    w_key,
    w_value,
    w_output,
):
    full_query, full_key, full_value, full_output = (
        lax.all_gather(w_query, "shard", axis=0, tiled=True),
        lax.all_gather(w_key, "shard", axis=0, tiled=True),
        lax.all_gather(w_value, "shard", axis=0, tiled=True),
        lax.all_gather(w_output, "shard", axis=0, tiled=True),
    )
    owner, positions, token_weight = row_layout(lengths[0], levels[0], level_scale, tokens.shape[0])

    def branch(
        tokens_in, gain_in, gain_query, gain_key, proj_query, proj_key, proj_value, proj_output
    ):
        return layer_branch(
            tokens_in,
            gain_in,
            gain_query,
            gain_key,
            proj_query,
            proj_key,
            proj_value,
            proj_output,
            owner,
            positions,
        )

    _, pullback = jax.vjp(
        branch, tokens, norm_gain, q_gain, k_gain, full_query, full_key, full_value, full_output
    )
    gradients = pullback(cotangent.astype(jnp.float32) * token_weight[:, None])
    grad_tokens = gradients[0]
    shards = lax.axis_size("shard")
    groups = lax.axis_size("dp")
    factor = 1.0 / math.sqrt(tokens.shape[0] * shards * groups)
    gain_norm, gain_query, gain_key = lax.psum(
        (gradients[1], gradients[2], gradients[3]), ("dp", "shard")
    )
    local_query = gradients[4].astype(jnp.float32)
    local_key = gradients[5].astype(jnp.float32)
    local_value = gradients[6].astype(jnp.float32)
    local_output = gradients[7].astype(jnp.float32)
    pieces = (
        lax.psum_scatter(local_query, "shard", scatter_dimension=0, tiled=True),
        lax.psum_scatter(local_key, "shard", scatter_dimension=0, tiled=True),
        lax.psum_scatter(local_value, "shard", scatter_dimension=0, tiled=True),
        lax.psum_scatter(local_output, "shard", scatter_dimension=0, tiled=True),
    )
    summed = lax.psum((pieces[0], pieces[1], pieces[2], pieces[3]), "dp")
    return (
        grad_tokens,
        gain_norm * factor,
        gain_query * factor,
        gain_key * factor,
        summed[0] * factor,
        summed[1] * factor,
        summed[2] * factor,
        summed[3] * factor,
    )


def solution(mesh):
    in_specs = (
        P(("dp", "shard"), None),
        P(("dp", "shard"), None),
        P(("dp", "shard"), None),
        P(("dp", "shard"), None),
        P(),
        P(),
        P(),
        P(),
        P("shard", None),
        P("shard", None),
        P("shard", None),
        P("shard", None),
    )
    out_specs = (
        P(("dp", "shard"), None),
        P(),
        P(),
        P(),
        P("shard", None),
        P("shard", None),
        P("shard", None),
        P("shard", None),
    )
    return jax.shard_map(body, mesh=mesh, in_specs=in_specs, out_specs=out_specs, check_vma=False)
```

profile of v0, /device:TPU:1, one launch (start us, length us, event | category | flops | bytes accessed | tf_op | source)
XLA Modules:
  0.0 672.4 jit_solution(5944769159972489158)
XLA Ops:
  16.4 41.6 %all-gather.11.cloned.1.call-done = bf16[1024,1024]{1,0:T(8,128)(2,1)} async-done(((bf16[32,1024]{1,0:T(8,128)(2,1)}), bf16[1024,1024]{1,0:T(8,128)(2,1)}) %all-gather.11.cloned.1.call-update) | async-done | bytes 2097168 | tf_op jit(solution)/shard_map/all_gather | solution.py:98
  58.0 2.9 fusion.27
  61.1 2.0 copy.127
  63.1 40.4 %all-gather.7.cloned.1.call-done = bf16[1024,1024]{1,0:T(8,128)(2,1)} async-done(((bf16[32,1024]{1,0:T(8,128)(2,1)}), bf16[1024,1024]{1,0:T(8,128)(2,1)}) %all-gather.7.cloned.1.call-update) | async-done | bytes 2097168 | tf_op jit(solution)/shard_map/all_gather | solution.py:97
  103.5 2.9 convolution_bitcast_fusion
  110.1 2.2 multiply_reduce_fusion.5
  114.6 36.8 %all-gather.5.cloned.1.call-done = bf16[2048,1024]{1,0:T(8,128)(2,1)} async-done(((bf16[64,1024]{1,0:T(8,128)(2,1)}), bf16[2048,1024]{1,0:T(8,128)(2,1)}) %all-gather.5.cloned.1.call-update) | async-done | bytes 4194320 | tf_op jit(solution)/shard_map/all_gather | solution.py:99
  151.4 6.3 convolution_convert_fusion.1
  157.7 3.9 copy.129
  161.6 37.7 %all-gather.9.cloned.1.call-done = bf16[1024,2048]{1,0:T(8,128)(2,1)} async-done(((bf16[32,2048]{1,0:T(8,128)(2,1)}), bf16[1024,2048]{1,0:T(8,128)(2,1)}) %all-gather.9.cloned.1.call-update) | async-done | bytes 4194320 | tf_op jit(solution)/shard_map/all_gather | solution.py:96
  199.3 7.0 %multiply_reduce_fusion.2 = (f32[512,16]{0,1:T(8,128)S(1)}, f32[512,2048]{0,1:T(8,128)}) fusion(bf16[1024,2048]{1,0:T(8,128)(2,1)} %all-gather.9.cloned.1.call-done, bf16[512,1024]{1,0:T(8,128)(2,1)} %param.12, f32[1024]{0:T(1024)S(1)} %copy-done.28, f32[512]{0:T(512)S(1)} %fusion.37), kind=kOutput, calls=%fused_computation.27 | convolution fusion | flops 2151669760 | bytes 9476096 | tf_op jit(solution)/shard_map/jvp()/reshape | solution.py:57
  206.9 3.2 multiply_multiply_fusion
  213.7 7.6 %fusion.7 = (f32[8,2,512]{2,1,0:T(2,128)S(1)}, f32[8,512,512,2]{2,1,3,0:T(8,128)}) fusion(pred[512,512]{0,1:T(8,128)(4,1)S(1)} %copy-done.10, bf16[512,8,128,1]{0,2,3,1:T(8,128)(2,1)S(1)} %fusion.30, bf16[512,8,2,128]{0,3,2,1:T(8,128)(2,1)S(1)} %fusion.10), kind=kOutput, calls=%fused_computation.12 | convolution fusion | flops 1086316544 | bytes 20217856 | tf_op jit(solution)/shard_map/jvp(tkgd,skd->kgts)/dot_general | solution.py:68
  221.3 9.2 %fusion.8 = f32[8,2,512]{2,1,0:T(2,128)S(1)} fusion(f32[8,512,512,2]{2,1,3,0:T(8,128)} %get-tuple-element.38, f32[8,2,512]{2,1,0:T(2,128)S(1)} %get-tuple-element.37, pred[512,512]{0,1:T(8,128)(4,1)} %copy.107), kind=kLoop, calls=%fused_computation.13 | loop fusion | flops 16769024 | bytes 17104896 | tf_op jit(solution)/shard_map/jvp()/reduce_sum | solution.py:75
  230.6 14.5 %divide_convert_fusion = (bf16[8,2,512,512]{2,3,1,0:T(8,128)(2,1)}, f32[8,2,512]{2,1,0:T(2,128)}, bf16[8,2,512,512]{2,3,1,0:T(8,128)(2,1)}) fusion(f32[8,512,512,2]{2,1,3,0:T(8,128)} %get-tuple-element.38, f32[8,2,512]{2,1,0:T(2,128)S(1)} %fusion.8, f32[8,2,512]{2,1,0:T(2,128)S(1)} %get-tuple-element.37, pred[512,512]{0,1:T(8,128)(4,1)} %copy.107, ...), kind=kOutput, calls=%fused_computation.10 | convolution fusion | flops 1115676672 | bytes 37093376 | tf_op jit(solution)/shard_map/transpose(jvp(kgts,skd->tkgd))/dot_general | solution.py:76
  245.0 6.3 bitcast_convert_fusion.1
  252.3 3.4 convert_convert_fusion.2
  255.8 11.7 %fusion.4 = bf16[8,512,512,2]{2,1,3,0:T(8,128)(2,1)S(1)} fusion(bf16[8,2,512,512]{2,3,1,0:T(8,128)(2,1)} %get-tuple-element.39, f32[8,512,512,2]{2,1,3,0:T(8,128)} %get-tuple-element.38, f32[8,512,2]{1,2,0:T(2,128)S(1)} %bitcast.151, f32[8,512,2]{1,2,0:T(2,128)} %negate_bitcast_fusion, f32[8,512,2]{1,2,0:T(2,128)S(1)} %bitcast.152, ...), kind=kLoop, calls=%fused_computation.6 | loop fusion | flops 41943040 | bytes 33914880 | tf_op jit(solution)/shard_map/transpose(jvp())/mul | solution.py:69
  267.5 2.8 bitcast_convert_fusion
  274.5 3.4 convert_convert_fusion.3
  278.9 4.9 bitcast_multiply_fusion
  286.1 2.2 multiply_reduce_fusion
  291.5 5.9 convert_convert_fusion.1
  298.6 5.0 convolution_convert_fusion.2
  303.6 5.7 convert_convert_fusion
  309.7 3.4 fusion.48
  316.1 2.9 fusion.21
  319.0 64.4 %all-reduce.4 = (f32[1024]{0:T(1024)S(1)}, f32[128]{0:T(128)S(1)}, f32[128]{0:T(128)S(1)}) all-reduce(f32[1024]{0:T(1024)S(1)} %get-tuple-element.12, f32[128]{0:T(128)S(1)} %get-tuple-element.8, f32[128]{0:T(128)S(1)} %get-tuple-element.10), channel_id=1, replica_groups=mesh['dp'=4,'shard'=32] {'dp','shard'}, use_global_device_ids=true, to_apply=%region_15.16 | all-reduce | flops 1280 | bytes 10240 | tf_op jit(solution)/shard_map/psum | solution.py:127
  383.9 36.6 %reduce-scatter.7.cloned.1.call-done = f32[32,1024]{1,0:T(8,128)} async-done(((f32[1024,1024]{1,0:T(8,128)}), f32[32,1024]{1,0:T(8,128)}) %reduce-scatter.7.cloned.1.call-update) | async-done | bytes 131088 | tf_op jit(solution)/shard_map/reduce_scatter | solution.py:136
  420.5 95.8 %reduce-scatter.5.cloned.1.call-done = f32[32,2048]{1,0:T(8,128)} async-done(((f32[1024,2048]{1,0:T(8,128)}), f32[32,2048]{1,0:T(8,128)}) %reduce-scatter.5.cloned.1.call-update) | async-done | bytes 262160 | tf_op jit(solution)/shard_map/reduce_scatter | solution.py:135
  516.3 96.2 %reduce-scatter.11.cloned.1.call-done = f32[64,1024]{1,0:T(8,128)} async-done(((f32[2048,1024]{1,0:T(8,128)}), f32[64,1024]{1,0:T(8,128)}) %reduce-scatter.11.cloned.1.call-update) | async-done | bytes 262160 | tf_op jit(solution)/shard_map/reduce_scatter | solution.py:138
  615.4 43.5 %all-reduce.8.cloned.1.call-done = (f32[32,2048]{1,0:T(8,128)}, f32[32,1024]{1,0:T(8,128)}, f32[32,1024]{1,0:T(8,128)}, f32[64,1024]{1,0:T(8,128)}) async-done(((f32[32,2048]{1,0:T(8,128)}, f32[32,1024]{1,0:T(8,128)}, f32[32,1024]{1,0:T(8,128)}, f32[64,1024]{1,0:T(8,128)}), (f32[32,2048]{1,0:T(8,128)}, f32[32,1024]{1,0:T(8,128)}, f32[32,1024]{1,0:T(8,128)}, ...) | async-done | bytes 786448 | tf_op jit(solution)/shard_map/psum | solution.py:140
  (132 shorter events, 45.4 us)
Async XLA Ops:
  7.2 8.9 %copy-start.11 = (bf16[512,1024]{1,0:T(8,128)(2,1)S(1)}, bf16[512,1024]{1,0:T(8,128)(2,1)}, u32[]{:S(2)}) copy-start(bf16[512,1024]{1,0:T(8,128)(2,1)} %param.12) | copy-start | bytes 3145732
  7.2 50.8 %copy-start.28 = (f32[1024]{0:T(1024)S(1)}, f32[1024]{0:T(1024)}, u32[]{:S(2)}) copy-start(f32[1024]{0:T(1024)} %param.17) | copy-start | bytes 12292
  7.2 50.8 %all-gather.11.cloned.1.call-start = ((), (), s32[]{:S(2)}) async-start(), calls=%async_computation.7 | async-start | bytes 2162688 | tf_op jit(solution)/shard_map/all_gather | solution.py:98
  7.9 95.6 %all-gather.7.cloned.1.call-start = ((), (), s32[]{:S(2)}) async-start(), calls=%async_computation.5 | async-start | bytes 2162688 | tf_op jit(solution)/shard_map/all_gather | solution.py:97
  8.7 142.7 %all-gather.5.cloned.1.call-start = ((), (), s32[]{:S(2)}) async-start(), calls=%async_computation.4 | async-start | bytes 4325376 | tf_op jit(solution)/shard_map/all_gather | solution.py:99
  9.4 189.8 %all-gather.9.cloned.1.call-start = ((), (), s32[]{:S(2)}) async-start(), calls=%async_computation.6 | async-start | bytes 4325376 | tf_op jit(solution)/shard_map/all_gather | solution.py:96
  10.0 373.9 %reduce-scatter.9.cloned.1.call-start = ((), (), s32[]{:S(2)}) async-start(), calls=%async_computation.10 | async-start | bytes 4325376 | tf_op jit(solution)/shard_map/reduce_scatter | solution.py:137
  110.1 2.4 copy-start.26
  161.6 45.3 %copy-start.25 = (f32[128]{0:T(128)S(1)}, f32[128]{0:T(128)}, u32[]{:S(2)}) copy-start(f32[128]{0:T(128)} %param.18) | copy-start | bytes 1540
  210.1 2.2 copy-start
  210.2 2.2 copy-start.7
  213.7 7.6 %copy-start.4 = (bf16[512,8,2,128]{0,3,2,1:T(8,128)(2,1)}, bf16[512,8,2,128]{0,3,2,1:T(8,128)(2,1)S(1)}, u32[]{:S(2)}) copy-start(bf16[512,8,2,128]{0,3,2,1:T(8,128)(2,1)S(1)} %fusion.10) | copy-start | bytes 6291460
  230.6 14.5 %copy-start.3 = (bf16[512,2048]{0,1:T(8,128)(2,1)S(1)}, bf16[512,2048]{0,1:T(8,128)(2,1)}, u32[]{:S(2)}) copy-start(bf16[512,2048]{0,1:T(8,128)(2,1)} %copy.129) | copy-start | bytes 6291460
  245.0 6.3 copy-start.24
  245.0 7.3 %copy-start.12 = (bf16[512,1024]{1,0:T(8,128)(2,1)S(1)}, bf16[512,1024]{1,0:T(8,128)(2,1)}, u32[]{:S(2)}) copy-start(bf16[512,1024]{1,0:T(8,128)(2,1)} %param.12) | copy-start | bytes 3145732
  245.0 7.3 %copy-start.29 = (f32[1024]{0:T(1024)S(1)}, f32[1024]{0:T(1024)}, u32[]{:S(2)}) copy-start(f32[1024]{0:T(1024)} %param.17) | copy-start | bytes 12292
  255.8 164.7 %reduce-scatter.7.cloned.1.call-start = ((), (), s32[]{:S(2)}) async-start(), calls=%async_computation.9 | async-start | bytes 4325376 | tf_op jit(solution)/shard_map/reduce_scatter | solution.py:136
  255.8 11.7 %copy-start.5 = (bf16[512,8,2,128]{0,3,2,1:T(8,128)(2,1)S(1)}, bf16[512,8,2,128]{0,3,2,1:T(8,128)(2,1)}, u32[]{:S(2)}) copy-start(bf16[512,8,2,128]{0,3,2,1:T(8,128)(2,1)} %copy-done.4) | copy-start | bytes 6291460
  267.5 3.2 copy-start.2
  267.5 3.2 copy-start.8
  272.6 1.9 copy-start.13
  272.6 1.8 copy-start.30
  277.9 238.3 %reduce-scatter.5.cloned.1.call-start = ((), (), s32[]{:S(2)}) async-start(), calls=%async_computation.8 | async-start | bytes 8650752 | tf_op jit(solution)/shard_map/reduce_scatter | solution.py:135
  283.8 2.3 copy-start.1
  286.1 2.2 copy-start.23
  288.4 3.1 copy-start.14
  297.4 6.2 copy-start.20
  297.4 315.2 %reduce-scatter.11.cloned.1.call-start = ((), (), s32[]{:S(2)}) async-start(), calls=%async_computation.11 | async-start | bytes 8650752 | tf_op jit(solution)/shard_map/reduce_scatter | solution.py:138
  309.3 3.8 copy-start.17
  309.3 349.6 %all-reduce.8.cloned.1.call-start = ((), (), s32[]{:S(2)}) async-start(), calls=%async_computation.12 | async-start | bytes 1572864 | tf_op jit(solution)/shard_map/psum | solution.py:140
  309.7 3.4 copy-start.32
  313.1 3.0 copy-start.31
  (10 other events, 10.7 us)
Sparse Core Ops, SparseCore 0:
  10.3 47.6 all-gather.10
  60.2 43.2 all-gather.6
  105.7 45.6 all-gather.4
  153.5 45.6 all-gather.8
  255.9 79.5 reduce-scatter.8
  339.4 81.0 reduce-scatter.6
  424.2 92.0 reduce-scatter.4
  520.5 92.0 reduce-scatter.10
  615.1 43.7 all-reduce.7
where the time goes:
time: 677 us; the launch traced here: 672 us
  waiting for transfers between devices  431 us (64%)
  matrix products  86.1 us (13%)
  blocking collectives  64.4 us (10%)
  other arithmetic  52.5 us (8%)
  local copies, waits for them, and re-layouts  22.7 us (3%)
  between operations  14.9 us (2%)
    reduce_scatter x1, waiting for transfers between devices, body(): lax.psum_scatter(local_output, 'shard', scatter_dimension=0, tiled=True)  96.2 us
    reduce_scatter x1, waiting for transfers between devices, body(): lax.psum_scatter(local_query, 'shard', scatter_dimension=0, tiled=True)  95.8 us
    psum x1, blocking collectives, body(): lax.psum((gradients[1], gradients[2], gradients[3]), ('dp', 'shard'))  64.4 us
    psum x1, waiting for transfers between devices, body(): summed = lax.psum((pieces[0], pieces[1], pieces[2], pieces[3]), 'dp')  43.5 us
    all_gather x1, waiting for transfers between devices, body(): lax.all_gather(w_value, 'shard', axis=0, tiled=True)  41.6 us
    all_gather x1, waiting for transfers between devices, body(): lax.all_gather(w_key, 'shard', axis=0, tiled=True)  40.4 us
    all_gather x1, waiting for transfers between devices, body(): lax.all_gather(w_query, 'shard', axis=0, tiled=True)  37.7 us
    all_gather x1, waiting for transfers between devices, body(): lax.all_gather(w_output, 'shard', axis=0, tiled=True)  36.8 us
  transfers between devices with their start and end apart: 9, of which 8 were waited for; matrix products, arithmetic and copies ran while one was open for 13% of the time, Pallas kernels for 0%

commit v1 on v0

v1 whole, which is shorter than its diff:
```python
import functools
import math

import jax
import jax.numpy as jnp
from jax import lax
from jax.experimental import pallas as pl
from jax.experimental.pallas import tpu as pltpu
from jax.sharding import Mesh
from jax.sharding import PartitionSpec as P

norm_eps = 1e-06
rope_theta = 1000000.0
HD = 128
T = 512
D = 1024
HALF = T // 2
NEG = -1e30
LOG2E = 1.4426950408889634
SCALE = 1.0 / math.sqrt(HD)
ALL = ("dp", "z", "y", "core")
VMEM_LIMIT = 56 * 1024 * 1024
BF = jnp.bfloat16
F32 = jnp.float32


COST = pl.CostEstimate(flops=1024, bytes_accessed=1024, transcendentals=0)


def params(**kw):
    return pltpu.CompilerParams(vmem_limit_bytes=VMEM_LIMIT, **kw)


def shift(x, axis, by):
    n = lax.axis_size(axis)
    return lax.ppermute(x, axis, [(i, (i + by) % n) for i in range(n)])


def swap(x):
    return lax.ppermute(x, "core", [(0, 1), (1, 0)])


def dot_nt(a, b):
    return lax.dot_general(a, b, (((1,), (1,)), ((), ())), preferred_element_type=F32)


def dot_tn(a, b):
    return lax.dot_general(a, b, (((0,), (0,)), ((), ())), preferred_element_type=F32)


def row_layout(lengths, levels, level_scale):
    ends = jnp.cumsum(lengths, axis=1)
    starts = ends - lengths
    places = jnp.arange(T, dtype=jnp.int32)
    owner = jnp.sum((places[None, :, None] >= ends[:, None, :]).astype(jnp.int32), axis=2)
    slots = jnp.arange(lengths.shape[1], dtype=jnp.int32)
    member = owner[:, :, None] == slots[None, None, :]
    positions = places[None, :] - jnp.sum(jnp.where(member, starts[:, None, :], 0), axis=2)
    hit = levels[:, :, None] == jnp.arange(level_scale.shape[0], dtype=jnp.int32)[None, None, :]
    slot_weight = jnp.sum(jnp.where(hit, level_scale[None, None, :], F32(0.0)), axis=2)
    slot_weight = jnp.where(slots[None, :] < lengths.shape[1] - 1, slot_weight, F32(0.0))
    weight = jnp.sum(jnp.where(member, slot_weight[:, None, :], F32(0.0)), axis=2)
    return positions, weight


def cross(x, by, turned):
    pairs = []
    for z in range(4):
        for y in range(4):
            for c in range(2):
                along_z = (c == 0) != turned
                to_z, to_y = ((z + by) % 4, y) if along_z else (z, (y + by) % 4)
                pairs.append(((z * 4 + y) * 2 + c, (to_z * 4 + to_y) * 2 + c))
    return lax.ppermute(x, ("z", "y", "core"), pairs)


def gather_line(x, turned):
    far, nxt, prv = cross(x, 2, turned), cross(x, -1, turned), cross(x, 1, turned)
    return [x, nxt, far, prv]


def send_line(pieces, turned):
    own, nxt, far, prv = pieces
    far, nxt, prv = cross(far, 2, turned), cross(nxt, 1, turned), cross(prv, -1, turned)
    return [own, nxt, prv, far]


def row_of(ids, r, s):
    z, y, core = ids[0], ids[1], ids[2]
    to = lax.rem(z + r + core * (s - r), 4) * 256 + lax.rem(y + s + core * (r - s), 4) * 64
    return pl.ds(pl.multiple_of(to, 64), 64)


SMEM = pl.BlockSpec(memory_space=pltpu.SMEM)
VM = pl.BlockSpec(memory_space=pltpu.VMEM)
ANY = pl.BlockSpec(memory_space=pl.ANY)
GROUP = 4 * HD
WIDTH = 4 * GROUP
WIDE = WIDTH + HD


def simple(kernel, name, shapes, *args):
    return pl.pallas_call(
        kernel,
        in_specs=[SMEM] + [VM] * (len(args) - 1),
        out_specs=[VM] * len(shapes),
        out_shape=[jax.ShapeDtypeStruct(shape, BF) for shape in shapes],
        compiler_params=params(),
        cost_estimate=COST,
        name=name,
    )(*args)


def cut_kernel(ids, wq, wk, wv, slots, mine, send):
    for out, half in ((mine, ids[2]), (send, 1 - ids[2])):
        for h in range(4):
            at = GROUP * h
            out[0:32, at : at + 256] = wq[:, pl.ds(pl.multiple_of(half * 1024 + 256 * h, HD), 256)]
            out[0:32, at + 256 : at + 384] = wk[:, pl.ds(pl.multiple_of(half * 512 + HD * h, HD), HD)]
            out[0:32, at + 384 : at + 512] = wv[:, pl.ds(pl.multiple_of(half * 512 + HD * h, HD), HD)]
    send[32:48, :HD] = slots[...]
    send[32:48, HD:] = jnp.zeros((16, WIDTH - HD), BF)


def join_kernel(ids, mine, came, wo, block):
    at = ids[2] * 32
    block[pl.ds(pl.multiple_of(at, 32), 32), :WIDTH] = mine[...]
    block[pl.ds(pl.multiple_of(32 - at, 32), 32), :WIDTH] = came[0:32, :]
    block[:, WIDTH:] = wo[...]


def stack_kernel(ids, p0, p1, p2, p3, line, wo_line):
    for i, part in enumerate((p0, p1, p2, p3)):
        line[64 * i : 64 * i + 64, :] = part[:, :WIDTH]
        wo_line[64 * i : 64 * i + 64, :] = part[:, WIDTH:]


def lane_mean(x):
    return jnp.dot(x.astype(BF), jnp.full((HD, HD), 1.0 / HD, BF), preferred_element_type=F32)


def project_kernel(ids, normed, cos, sin, qg, kg, p0, p1, p2, p3, qkv, factors, w):
    for r, part in enumerate((p0, p1, p2, p3)):
        for s in range(4):
            w[row_of(ids, r, s), :] = part[64 * s : 64 * s + 64, :]
    chunks = [slice(HALF * i, HALF * (i + 1)) for i in range(normed.shape[0] // HALF)]
    lane = lax.broadcasted_iota(jnp.int32, (HALF, HD), 1)
    for rows in chunks:
        got = jnp.dot(normed[rows, :], w[...], preferred_element_type=F32)
        c, sn = cos[rows, :], sin[rows, :]
        kept = jnp.zeros((HALF, HD), F32)
        for i, gain in enumerate((qg, qg, kg)):
            x = got[:, HD * i : HD * (i + 1)]
            factor = lax.rsqrt(lane_mean(x * x) + norm_eps)
            high = factor.astype(BF).astype(F32)
            kept = jnp.where(lane == i, high, jnp.where(lane == i + 4, factor - high, kept))
            n = x * factor * gain[...]
            qkv[rows, HD * i : HD * (i + 1)] = (n * c + pltpu.roll(n, 64, 1) * sn).astype(BF)
        qkv[rows, 3 * HD :] = got[:, 3 * HD :].astype(BF)
        factors[rows, :] = kept.astype(BF)


def project(ids, normed, cos, sin, qg, kg, parts):
    rows = normed.shape[0]

    def whole(shape):
        return pl.BlockSpec(shape, lambda h: (0, 0))

    def by_head(rows, cols=GROUP):
        return pl.BlockSpec((rows, cols), lambda h: (0, h))

    return pl.pallas_call(
        project_kernel,
        grid=(4,),
        in_specs=[SMEM, whole((rows, D)), whole((rows, HD)), whole((rows, HD)), whole((1, HD)), whole((1, HD))] + [by_head(256)] * 4,
        out_specs=[by_head(rows), by_head(rows, HD), by_head(D)],
        out_shape=[
            jax.ShapeDtypeStruct((rows, WIDTH), BF),
            jax.ShapeDtypeStruct((rows, 4 * HD), BF),
            jax.ShapeDtypeStruct((D, WIDTH), BF),
        ],
        compiler_params=params(),
        cost_estimate=COST,
        name="project",
    )(ids, normed, cos, sin, qg, kg, *parts)


def fill_bias(start, bias):
    s = lax.broadcasted_iota(jnp.int32, (T, T), 0)
    t = lax.broadcasted_iota(jnp.int32, (T, T), 1)
    bias[...] = jnp.where((s >= start[0]) & (s <= t), F32(0.0), F32(NEG))


TILES = ((0, HALF, HALF), (HALF, T, T))
STEP = 128
PER = 2
REACH = [range(max(0, i - 2), i + 1) for i in range(T // STEP)]


def span(i):
    return slice(i * STEP, (i + 1) * STEP)


def columns(n, of):
    at = GROUP * (n // 2) + {"q": HD * (n % 2), "k": 2 * HD, "v": 3 * HD}[of]
    return slice(at, at + HD)


def forward_kernel(ids, qkv, start, keep, send, lse, bias, scores, probs):
    @pl.when((pl.program_id(0) == 0) & (pl.program_id(1) == 0))
    def _():
        probs[...] = jnp.zeros_like(probs)

    @pl.when(pl.program_id(1) == 0)
    def _():
        fill_bias(start, bias)

    def score(n):
        for lo, hi, keys in TILES:
            scores[n, :keys, lo:hi] = dot_nt(qkv[:keys, columns(n, "k")], qkv[lo:hi, columns(n, "q")])

    score(0)
    parts = []
    for n in range(2 * PER):
        if n + 1 < 2 * PER:
            score(n + 1)
        inverse = []
        for i, reach in enumerate(REACH):
            top = None
            for j in reach:
                x = scores[n, span(j), span(i)] * F32(SCALE * LOG2E) + bias[span(j), span(i)]
                scores[n, span(j), span(i)] = x
                top = x if top is None else jnp.maximum(top, x)
            top = jnp.max(top, axis=0, keepdims=True)
            total = None
            for j in reach:
                p = jnp.exp2(scores[n, span(j), span(i)] - top)
                probs[n, span(j), span(i)] = p.astype(BF)
                total = p if total is None else total + p
            total = jnp.sum(total, axis=0, keepdims=True)
            lse[n // 2, n % 2 : n % 2 + 1, span(i)] = top + jnp.log2(total)
            inverse.append(1.0 / total)
        tiles = [dot_tn(qkv[:keys, columns(n, "v")], probs[n, :keys, lo:hi]) for lo, hi, keys in TILES]
        parts.append(jnp.concatenate(tiles, axis=1) * jnp.concatenate(inverse, axis=1))
    core = ids[2]
    for m in range(PER):
        a, b = parts[2 * m : 2 * m + 2]
        low = jnp.concatenate([a[:64], b[:64]], axis=0).T.astype(BF)
        high = jnp.concatenate([a[64:], b[64:]], axis=0).T.astype(BF)
        cols = slice(HD * m, HD * (m + 1))

        @pl.when(core == 0)
        def _():
            keep[:, cols] = low
            send[:, cols] = high

        @pl.when(core == 1)
        def _():
            keep[:, cols] = high
            send[:, cols] = low


def attend(ids, qkv, start):
    rows = qkv.shape[0] // T
    heads = qkv.shape[1] // GROUP
    steps = heads // PER
    half = jax.ShapeDtypeStruct((rows * T, heads * HD), BF)
    tile = pl.BlockSpec((T, PER * HD), lambda r, h: (r, h))
    return pl.pallas_call(
        forward_kernel,
        grid=(rows, steps),
        in_specs=[SMEM, pl.BlockSpec((T, PER * GROUP), lambda r, h: (r, h)), pl.BlockSpec((1, 1, T), lambda r, h: (r, 0, 0))],
        out_specs=[tile, tile, pl.BlockSpec((PER, 2, T), lambda r, h: (r * steps + h, 0, 0))],
        out_shape=[half, half, jax.ShapeDtypeStruct((rows * heads, 2, T), F32)],
        scratch_shapes=[pltpu.VMEM((T, T), F32), pltpu.VMEM((2 * PER, T, T), F32), pltpu.VMEM((2 * PER, T, T), BF)],
        compiler_params=params(),
        cost_estimate=COST,
        name="attend",
    )(ids, qkv, start)


def backward_kernel(
    ids, qkv, dm_a, dm_b, lse, factors, cos, sin, qg, kg, start, du, gq_out, gk_out, bias, low, high, dms, scores, dprobs, probs, dscores
):
    first = (pl.program_id(0) == 0) & (pl.program_id(1) == 0)

    @pl.when(first)
    def _():
        gq_out[...] = jnp.zeros_like(gq_out)
        gk_out[...] = jnp.zeros_like(gk_out)
        probs[...] = jnp.zeros_like(probs)
        dscores[...] = jnp.zeros_like(dscores)

    @pl.when(pl.program_id(1) == 0)
    def _():
        fill_bias(start, bias)

    @pl.when(ids[2] == 0)
    def _():
        low[...] = dm_a[...].astype(F32)
        high[...] = dm_b[...].astype(F32)

    @pl.when(ids[2] == 1)
    def _():
        low[...] = dm_b[...].astype(F32)
        high[...] = dm_a[...].astype(F32)

    c, sn = cos[...], sin[...]

    def unturn(grad, turned, at, gain):
        g = grad * c - pltpu.roll(grad, 64, 1) * sn
        turned = turned.astype(F32)
        gained = turned * c - pltpu.roll(turned, 64, 1) * sn
        product = g * gained
        group = slice(HD * (at // 4), HD * (at // 4 + 1))
        lanes = lax.broadcasted_iota(jnp.int32, (HD, HD), 0) % 8
        pick = jnp.where((lanes == at % 4) | (lanes == at % 4 + 4), F32(1.0), F32(0.0)).astype(BF)
        factor = jnp.dot(factors[:, group], pick, preferred_element_type=F32)
        back = factor * (g * gain - gained * (1.0 / gain) * lane_mean(product))
        return back.astype(BF), jnp.sum(product, axis=0, keepdims=True)

    lane = lax.broadcasted_iota(jnp.int32, (T, HD), 1)
    for m in range(PER):
        lo, hi = low[:, HD * m : HD * (m + 1)], high[:, HD * m : HD * (m + 1)]
        dms[2 * m] = jnp.where(lane < 64, lo, pltpu.roll(hi, 64, 1)).astype(BF)
        dms[2 * m + 1] = jnp.where(lane < 64, pltpu.roll(lo, 64, 1), hi).astype(BF)

    def score(n):
        for lo, hi, keys in TILES:
            scores[n, :keys, lo:hi] = dot_nt(qkv[:keys, columns(n, "k")], qkv[lo:hi, columns(n, "q")])
            dprobs[n, :keys, lo:hi] = dot_nt(qkv[:keys, columns(n, "v")], dms[n, lo:hi])

    score(0)
    gq = jnp.zeros((1, HD), F32)
    gk = jnp.zeros((1, HD), F32)
    dk = dv = None
    for n in range(2 * PER):
        if n + 1 < 2 * PER:
            score(n + 1)
        for i, reach in enumerate(REACH):
            level = lse[n // 2, n % 2 : n % 2 + 1, span(i)]
            mean = None
            for j in reach:
                p = jnp.exp2(scores[n, span(j), span(i)] * F32(SCALE * LOG2E) + bias[span(j), span(i)] - level)
                scores[n, span(j), span(i)] = p
                probs[n, span(j), span(i)] = p.astype(BF)
                p = p * dprobs[n, span(j), span(i)]
                mean = p if mean is None else mean + p
            mean = jnp.sum(mean, axis=0, keepdims=True)
            for j in reach:
                ds = scores[n, span(j), span(i)] * (dprobs[n, span(j), span(i)] - mean)
                dscores[n, span(j), span(i)] = ds.astype(BF)
        if n % 2 == 0:
            dk, dv = [0.0, 0.0], [0.0, 0.0]
        q = columns(n, "q")
        dq = jnp.concatenate([dot_tn(qkv[:keys, columns(n, "k")], dscores[n, :keys, lo:hi]) for lo, hi, keys in TILES], axis=1).T
        for i in range(2):
            keys, queries = slice(i * HALF, (i + 1) * HALF), slice(i * HALF, T)
            dk[i] += jnp.dot(dscores[n, keys, queries], qkv[queries, q], preferred_element_type=F32)
            dv[i] += jnp.dot(probs[n, keys, queries], dms[n, queries], preferred_element_type=F32)
        du[:, q], more = unturn(dq * F32(SCALE), qkv[:, q], 4 * (n // 2) + n % 2, qg[...])
        gq = gq + more
        if n % 2 == 1:
            k = columns(n, "k")
            du[:, k], more = unturn(jnp.concatenate(dk, axis=0) * F32(SCALE), qkv[:, k], 4 * (n // 2) + 2, kg[...])
            gk = gk + more
            du[:, columns(n, "v")] = jnp.concatenate(dv, axis=0).astype(BF)
    gq_out[...] += gq / qg[...]
    gk_out[...] += gk / kg[...]


def attend_back(ids, qkv, dm_a, dm_b, lse, factors, cos, sin, qg, kg, start):
    rows = qkv.shape[0] // T
    heads = qkv.shape[1] // GROUP
    steps = heads // PER

    def tile(cols):
        return pl.BlockSpec((T, PER * cols), lambda r, h: (r, h))

    by_row = pl.BlockSpec((T, HD), lambda r, h: (r, 0))
    gain = pl.BlockSpec((1, HD), lambda r, h: (0, 0))
    gain_shape = jax.ShapeDtypeStruct((1, HD), F32)
    return pl.pallas_call(
        backward_kernel,
        grid=(rows, steps),
        in_specs=[
            SMEM,
            tile(GROUP),
            tile(HD),
            tile(HD),
            pl.BlockSpec((PER, 2, T), lambda r, h: (r * steps + h, 0, 0)),
            tile(HD),
            by_row,
            by_row,
            gain,
            gain,
            pl.BlockSpec((1, 1, T), lambda r, h: (r, 0, 0)),
        ],
        out_specs=[tile(GROUP), gain, gain],
        out_shape=[jax.ShapeDtypeStruct((rows * T, heads * GROUP), BF), gain_shape, gain_shape],
        scratch_shapes=[pltpu.VMEM((T, T), F32), pltpu.VMEM((T, PER * HD), F32), pltpu.VMEM((T, PER * HD), F32)]
        + [pltpu.VMEM((2 * PER, T, HD), BF)]
        + [pltpu.VMEM((2 * PER, T, T), kind) for kind in (F32, F32, BF, BF)],
        compiler_params=params(),
        cost_estimate=COST,
        name="attend_back",
    )(ids, qkv, dm_a, dm_b, lse, factors, cos, sin, qg, kg, start)


def to_mixed_kernel(ids, cot, p0, p1, p2, p3, keep, send, wo):
    @pl.when(pl.program_id(0) == 0)
    def _():
        for r, part in enumerate((p0, p1, p2, p3)):
            for s in range(4):
                wo[row_of(ids, r, s), :] = part[64 * s : 64 * s + 64, :]

    at = ids[2] * 512
    mine = wo[pl.ds(pl.multiple_of(at, 512), 512), :]
    theirs = wo[pl.ds(pl.multiple_of(512 - at, 512), 512), :]
    send[...] = dot_nt(cot[...], theirs).astype(BF)
    keep[...] = dot_nt(cot[...], mine).astype(BF)


def to_mixed(ids, cot, parts):
    rows = cot.shape[0]
    step = 512

    def by_row(cols):
        return pl.BlockSpec((step, cols), lambda i: (i, 0))

    return pl.pallas_call(
        to_mixed_kernel,
        grid=(rows // step,),
        in_specs=[SMEM, by_row(D)] + [pl.BlockSpec((256, D), lambda i: (0, 0))] * 4,
        out_specs=[by_row(512)] * 2,
        out_shape=[jax.ShapeDtypeStruct((rows, 512), BF)] * 2,
        scratch_shapes=[pltpu.VMEM((D, D), BF)],
        compiler_params=params(),
        cost_estimate=COST,
        name="to_mixed",
    )(ids, cot, *parts)


def output_pieces_kernel(ids, keep, got, cot, o0, o1, o2, o3, mixed, res):
    core = ids[2]

    @pl.when((pl.program_id(0) == 0) & (core == 0))
    def _():
        mixed[:, :512] = keep[...]
        mixed[:, 512:] = got[...]

    @pl.when((pl.program_id(0) == 0) & (core == 1))
    def _():
        mixed[:, :512] = got[...]
        mixed[:, 512:] = keep[...]

    res[...] = dot_tn(mixed[...], cot[...]).astype(BF)
    for r, out in enumerate((o0, o1, o2, o3)):
        for s in range(4):
            out[64 * s : 64 * s + 64, :] = res[row_of(ids, r, s), :]


def output_pieces(ids, keep, got, cot):
    rows = cot.shape[0]
    step = 512

    def whole(shape):
        return pl.BlockSpec(shape, lambda i: (0, 0))

    return pl.pallas_call(
        output_pieces_kernel,
        grid=(D // step,),
        in_specs=[SMEM, whole(keep.shape), whole(got.shape), pl.BlockSpec((rows, step), lambda i: (0, i))],
        out_specs=[pl.BlockSpec((256, step), lambda i: (0, i))] * 4,
        out_shape=[jax.ShapeDtypeStruct((256, D), BF)] * 4,
        scratch_shapes=[pltpu.VMEM((rows, D), BF), pltpu.VMEM((D, step), BF)],
        compiler_params=params(),
        cost_estimate=COST,
        name="output_pieces",
    )(ids, keep, got, cot)


def pieces_kernel(ids, x, w, up, gq, gk, o0, o1, o2, o3, gain, last, res, left):
    h = pl.program_id(0)
    steps = pl.num_programs(0)
    outs = (o0, o1, o2, o3)

    def departures(h):
        slot = lax.rem(h, 2)
        cols = pl.ds(pl.multiple_of(h * GROUP, GROUP), GROUP)
        return [
            pltpu.make_async_copy(res.at[slot, row_of(ids, r, s), :], out.at[64 * s : 64 * s + 64, cols], left.at[slot])
            for r, out in enumerate(outs)
            for s in range(4)
        ]

    @pl.when(h == 0)
    def _():
        gain[...] = jnp.zeros_like(gain)
        last[...] = jnp.zeros_like(last)

    @pl.when(h >= 2)
    def _():
        for copy in departures(h - 2):
            copy.wait()

    every = dot_tn(x[...], up[...])
    for i in range(4):
        block = slice(256 * i, 256 * (i + 1))
        got = every[block, :]
        res[lax.rem(h, 2), block, :] = got.astype(BF)
        product = got * w[block, :].astype(F32)
        dots = product[:, :HD]
        for j in range(1, GROUP // HD):
            dots = dots + product[:, j * HD : (j + 1) * HD]
        dots = jnp.sum(dots.T, axis=0, keepdims=True)
        gain[2 * i : 2 * i + 1, :] += dots[:, :HD]
        gain[2 * i + 1 : 2 * i + 2, :] += dots[:, HD:]
    for copy in departures(h):
        copy.start()

    @pl.when(h == steps - 1)
    def _():
        gain[8:9, :] = gq[...]
        gain[9:10, :] = gk[...]
        last[0:16, :] = gain[...].astype(BF)
        extra = [pltpu.make_async_copy(last, out.at[:, WIDTH:], left.at[2]) for out in outs]
        for copy in extra:
            copy.start()
        for copy in departures(h - 1) + departures(h) + extra:
            copy.wait()


def weight_pieces(ids, x, w, up, gq, gk):
    rows = x.shape[0]
    piece = (256, WIDTH + HD)

    def whole(shape):
        return pl.BlockSpec(shape, lambda h: (0, 0))

    def by_head(rows):
        return pl.BlockSpec((rows, GROUP), lambda h: (0, h))

    return pl.pallas_call(
        pieces_kernel,
        grid=(4,),
        in_specs=[SMEM, whole(x.shape), by_head(D), by_head(rows), whole((1, HD)), whole((1, HD))],
        out_specs=[ANY] * 4,
        out_shape=[jax.ShapeDtypeStruct(piece, BF)] * 4,
        scratch_shapes=[
            pltpu.VMEM((16, HD), F32),
            pltpu.VMEM((256, HD), BF),
            pltpu.VMEM((2, D, GROUP), BF),
            pltpu.SemaphoreType.DMA((3,)),
        ],
        compiler_params=params(),
        cost_estimate=COST,
        name="weight_pieces",
    )(ids, x, w, up, gq, gk)


def to_normed_kernel(ids, du, w, theirs, own):
    got = dot_nt(du[...], w[...])

    @pl.when(pl.program_id(0) < 2)
    def _():
        theirs[...] = got.astype(BF)

    @pl.when(pl.program_id(0) >= 2)
    def _():
        own[...] = got


def to_normed(ids, du, w):
    def block(i, ids):
        row = jnp.where(i < 2, 1 - ids[2], ids[2])
        return (2 * row + lax.rem(i, 2), 0)

    return pl.pallas_call(
        to_normed_kernel,
        grid_spec=pltpu.PrefetchScalarGridSpec(
            num_scalar_prefetch=1,
            grid=(4,),
            in_specs=[pl.BlockSpec((HALF, WIDTH), block), pl.BlockSpec((D, WIDTH), lambda i, ids: (0, 0))],
            out_specs=[
                pl.BlockSpec((HALF, D), lambda i, ids: (jnp.minimum(i, 1), 0)),
                pl.BlockSpec((HALF, D), lambda i, ids: (jnp.maximum(i - 2, 0), 0)),
            ],
        ),
        out_shape=[jax.ShapeDtypeStruct((T, D), BF), jax.ShapeDtypeStruct((T, D), F32)],
        compiler_params=params(),
        cost_estimate=COST,
        name="to_normed",
    )(ids, du, w)


def added(parts, rows, cols=slice(None)):
    total = parts[0][rows, cols].astype(F32)
    for part in parts[1:]:
        total = total + part[rows, cols].astype(F32)
    return total


def add_split_kernel(ids, *refs):
    parts, parts_o, outs = refs[:4], refs[4:8], refs[8:]
    for s, out in enumerate(outs):
        rows = slice(64 * s, 64 * s + 64)
        out[:, :WIDTH] = added(parts, rows, slice(0, WIDTH)).astype(BF)
        out[:, WIDTH:WIDE] = added(parts, slice(0, 64), slice(WIDTH, WIDE)).astype(BF)
        out[:, WIDE:] = added(parts_o, rows).astype(BF)


def share_kernel(ids, a, b, c, d, keep, send):
    parts = (a, b, c, d)
    for out, at in ((keep, ids[2] * 32), (send, 32 - ids[2] * 32)):
        out[:, :WIDTH] = added(parts, pl.ds(pl.multiple_of(at, 32), 32), slice(0, WIDTH)).astype(BF)
        out[:, WIDTH:WIDE] = added(parts, slice(0, 32), slice(WIDTH, WIDE)).astype(BF)
    for i in range(2):
        at = WIDE + D * i
        keep[:, at : at + D] = added(parts, slice(32 * i, 32 * i + 32), slice(WIDE, WIDE + D)).astype(BF)


def finish_kernel(factor, ids, gain, a, b, c, d, dq, dk, dv, do, g_norm, g_query, g_key):
    parts = (a, b, c, d)
    every = slice(None)
    second = WIDE + 2 * D
    for begin, half in ((0, ids[2]), (second, 1 - ids[2])):
        for h in range(4):
            at = begin + GROUP * h
            dq[:, pl.ds(pl.multiple_of(half * 1024 + 256 * h, HD), 256)] = added(parts, every, slice(at, at + 256)) * factor
            to = pl.ds(pl.multiple_of(half * 512 + HD * h, HD), HD)
            dk[:, to] = added(parts, every, slice(at + 256, at + 384)) * factor
            dv[:, to] = added(parts, every, slice(at + 384, at + 512)) * factor
    for i in range(2):
        at = WIDE + D * i
        do[32 * i : 32 * i + 32, :] = added(parts, every, slice(at, at + D)) * factor
    gains = [added(parts, slice(0, 16), slice(at + WIDTH, at + WIDE)) for at in (0, second)]
    gains = (gains[0] + gains[1]) * factor
    g_norm[...] = gains[0:8] / gain[...]
    g_query[...] = gains[8:9]
    g_key[...] = gains[9:10]


def finish(ids, norm_gain, parts, factor):
    shapes = [(32, 2048), (32, 1024), (32, 1024), (64, 1024), (8, HD), (1, HD), (1, HD)]
    return pl.pallas_call(
        functools.partial(finish_kernel, factor),
        in_specs=[SMEM] + [VM] * 5,
        out_specs=[VM] * 7,
        out_shape=[jax.ShapeDtypeStruct(shape, F32) for shape in shapes],
        compiler_params=params(),
        cost_estimate=COST,
        name="finish",
    )(ids, norm_gain.reshape(8, HD), *parts)


def groups_line(x):
    return [x, shift(x, "dp", 2), shift(x, "dp", 1), shift(x, "dp", -1)]


def body(tokens, cotangent, lengths, levels, level_scale, norm_gain, q_gain, k_gain, w_query, w_key, w_value, w_output):
    core, z, y = lax.axis_index("core"), lax.axis_index("z"), lax.axis_index("y")
    first = core == 0
    ids = jnp.stack([z, y, core, core]).astype(jnp.int32)

    slots = jnp.concatenate([lengths, levels], 1)
    sent = jnp.pad(slots.astype(BF), ((0, 15), (0, HD - 8)))
    mine, send = simple(cut_kernel, "cut", [(32, WIDTH), (48, WIDTH)], ids, w_query, w_key, w_value, sent)
    came = swap(send)
    (block,) = simple(join_kernel, "join", [(64, WIDTH + D)], ids, mine, came, w_output)
    line, wo_line = simple(stack_kernel, "stack", [(256, WIDTH), (256, D)], ids, *gather_line(block, True))
    parts = gather_line(line, False)

    def pair(own, other):
        return jnp.where(first, jnp.concatenate([own, other], 0), jnp.concatenate([other, own], 0))

    slots = pair(slots, came[32:33, :8].astype(jnp.int32))
    tokens2 = pair(tokens, swap(tokens))
    positions, weight = row_layout(slots[:, :4], slots[:, 4:], level_scale)
    start = (jnp.arange(T, dtype=jnp.int32)[None, :] - positions)[:, None, :]
    weight = weight.reshape(2 * T, 1)
    freqs = rope_theta ** (-jnp.arange(HD // 2, dtype=F32) * 2.0 / HD)
    angles = positions.reshape(2 * T, 1).astype(F32) * freqs[None, :]
    cos, sin = jnp.cos(angles), jnp.sin(angles)
    cos = jnp.concatenate([cos, cos], 1)
    sin = jnp.concatenate([-sin, sin], 1)

    wide = tokens2.astype(F32)
    inverse = lax.rsqrt(jnp.mean(wide * wide, axis=-1, keepdims=True) + norm_eps)
    normed = (wide * inverse * norm_gain).astype(BF)
    qg, kg = q_gain[None, :], k_gain[None, :]

    cotw = (pair(cotangent, swap(cotangent)).astype(F32) * weight).astype(BF)
    parts, wo_line, normed, cotw, start = lax.optimization_barrier((parts, wo_line, normed, cotw, start))
    wo_parts = gather_line(wo_line, False)
    qkv, factors, w = project(ids, normed, cos, sin, qg, kg, parts)
    keep, send, lse = attend(ids, qkv, start)
    got = swap(send)
    dm_keep, dm_send = to_mixed(ids, cotw, wo_parts)
    dm_got = swap(dm_send)
    sum_o = send_line(output_pieces(ids, keep, got, cotw), False)
    du, gq, gk = attend_back(ids, qkv, dm_keep, dm_got, lse, factors, cos, sin, qg, kg, start)
    du, sum_o = lax.optimization_barrier((du, sum_o))
    pieces = weight_pieces(ids, normed, w, du, gq, gk)
    pieces, du = lax.optimization_barrier((pieces, du))
    total = send_line(pieces, False)
    theirs, back = to_normed(ids, du, w)
    halves = simple(add_split_kernel, "add_split", [(64, WIDE + D)] * 4, ids, *total, *sum_o)
    kept, send = simple(share_kernel, "share", [(32, WIDE + 2 * D), (32, WIDE)], ids, *send_line(halves, True))
    both = jnp.concatenate([kept, swap(send)], 1)
    factor = 1.0 / math.sqrt(T * 128)
    d_query, d_key, d_value, d_output, g_norm, g_query, g_key = finish(ids, norm_gain, groups_line(both), factor)

    hat = wide * inverse

    def own_row(x):
        return jnp.where(first, x[:T], x[T:])

    back, hat = back + swap(theirs).astype(F32), own_row(hat)
    scaled = back * norm_gain
    grad = own_row(inverse) * (scaled - hat * jnp.mean(scaled * hat, axis=-1, keepdims=True))
    grad_tokens = (grad + cotangent.astype(F32) * own_row(weight)).astype(BF)

    return grad_tokens, g_norm.reshape(D), g_query.reshape(HD), g_key.reshape(HD), d_query, d_key, d_value, d_output


def solution(mesh):
    mesh = Mesh(mesh.devices.reshape(4, 4, 4, 2), ALL)
    shard = ("z", "y", "core")
    rows = P(ALL, None)
    weights = P(shard, None)
    return jax.shard_map(
        body,
        mesh=mesh,
        in_specs=(rows,) * 4 + (P(),) * 4 + (weights,) * 4,
        out_specs=(rows, P(), P(), P()) + (weights,) * 4,
        check_vma=False,
    )
```

time: 677 us -> 211 us (0.31)
  waiting for transfers between devices: 431 us -> 56.9 us
  matrix products: 86.1 us -> 0 us
  Pallas kernels: 0 us -> 86.1 us
  blocking collectives: 64.4 us -> 0 us
  starting transfers between devices: 0.65 us -> 37.3 us
  other arithmetic: 52.5 us -> 21.2 us
  local copies, waits for them, and re-layouts: 22.7 us -> 8.23 us
  between operations: 14.9 us -> 0.89 us
    reduce_scatter x4 -> x0, waiting for transfers between devices: 229 us -> none  [the longest x1 96.2 us: body(): lax.psum_scatter(local_output, 'shard', scatter_dimension=0, tiled=True)]
    all_gather x4 -> x0, waiting for transfers between devices: 156 us -> none  [the longest x1 41.6 us: body(): lax.all_gather(w_value, 'shard', axis=0, tiled=True)]
    pallas_call x0 -> x13, Pallas kernels: none -> 86.1 us  [the longest x1 18.4 us: attend_back(): pl.pallas_call(backward_kernel, grid=(rows, steps), in_specs=[SMEM, tile(...]
    dot_general x16 -> x0, matrix products: 79.1 us -> none  [the longest x3 25.7 us: layer_branch(): jnp.einsum('kgts,skd->tkgd', probs, values_all, preferred_element_type=jn...]
    psum x1 -> x0, blocking collectives: 64.4 us -> none  [body(): lax.psum((gradients[1], gradients[2], gradients[3]), ('dp', 'shard'))]
    ppermute x0 -> x28, waiting for transfers between devices: none -> 56.9 us  [the longest x18 42.4 us: cross(): return lax.ppermute(x, ('z', 'y', 'core'), pairs)]
    psum x1 -> x0, waiting for transfers between devices: 43.5 us -> none  [body(): summed = lax.psum((pieces[0], pieces[1], pieces[2], pieces[3]), 'dp')]
    ppermute x0 -> x28, starting transfers between devices: none -> 37.3 us  [the longest x18 21.1 us: cross(): return lax.ppermute(x, ('z', 'y', 'core'), pairs)]
  transfers between devices with their start and end apart: 9 -> 28, of which waited for: 8 -> 11; matrix products, arithmetic and copies ran while one was open for 13% -> 10% of each run, Pallas kernels for 0% -> 33%
where the time goes in v1:
time: 211 us
  Pallas kernels  86.1 us (41%)
  waiting for transfers between devices  56.9 us (27%)
  starting transfers between devices  37.3 us (18%)
  other arithmetic  21.2 us (10%)
  local copies, waits for them, and re-layouts  8.23 us (4%)
    ppermute x18, waiting for transfers between devices, cross(): return lax.ppermute(x, ('z', 'y', 'core'), pairs)  42.4 us
    ppermute x18, starting transfers between devices, cross(): return lax.ppermute(x, ('z', 'y', 'core'), pairs)  21.1 us
    pallas_call x1, Pallas kernels, attend_back(): pl.pallas_call(backward_kernel, grid=(rows, steps), in_specs=[SMEM, tile(...  18.4 us
    ppermute x3, waiting for transfers between devices, shift(): return lax.ppermute(x, axis, [(i, (i + by) % n) for i in range(n)])  13.3 us
    pallas_call x5, Pallas kernels, simple(): pl.pallas_call(kernel, in_specs=[SMEM] + [VM] * (len(args) - 1), out_spec...  12.9 us
    pallas_call x1, Pallas kernels, project(): pl.pallas_call(project_kernel, grid=(4,), in_specs=[SMEM, whole((rows, D)...  12.5 us
    ppermute x7, starting transfers between devices, swap(): return lax.ppermute(x, 'core', [(0, 1), (1, 0)])  10.7 us
    pallas_call x1, Pallas kernels, weight_pieces(): pl.pallas_call(pieces_kernel, grid=(4,), in_specs=[SMEM, whole(x.shape),...  10.2 us
  transfers between devices with their start and end apart: 28, of which 11 were waited for; matrix products, arithmetic and copies ran while one was open for 10% of the time, Pallas kernels for 33%

profile of v1, /device:TPU:1, one launch (start us, length us, event | category | flops | bytes accessed | tf_op | source)
XLA Modules:
  0.0 210.7 jit_solution(11298941681635718025)
XLA Ops:
  9.8 3.8 %collective-permute-start.2 = (bf16[64,3072]{1,0:T(8,128)(2,1)}, bf16[64,3072]{1,0:T(8,128)(2,1)S(1)}, u32[]{:S(2)}, u32[]{:S(2)}) collective-permute-start(bf16[64,3072]{1,0:T(8,128)(2,1)} %join.1.p0), channel_id=1, source_target_pairs={{0,6},{1,25},{2,0},{3,27},{4,2},{5,29},{6,4},{7,31},{8,14},{9,1},{... | collective-permute-start | bytes 1179656 | tf_op jit(solution)/shard_map/ppermute | solution.py:74
  22.9 3.4 %collective-permute-done.4.p3 = bf16[64,3072]{1,0:T(8,128)(2,1)} collective-permute-done((bf16[64,3072]{1,0:T(8,128)(2,1)}, bf16[64,3072]{1,0:T(8,128)(2,1)}, u32[]{:S(2)}, u32[]{:S(2)}) %collective-permute-start.4) | collective-permute-done | bytes 393248 | tf_op jit(solution)/shard_map/ppermute | solution.py:74
  26.3 2.6 %stack.18 = (bf16[256,2048]{1,0:T(8,128)(2,1)}, bf16[256,1024]{1,0:T(8,128)(2,1)}) custom-call(s32[4]{0:T(128)} %pad_add_fusion.ids, bf16[64,3072]{1,0:T(8,128)(2,1)} %join.1.p0, bf16[64,3072]{1,0:T(8,128)(2,1)} %copy-done.17, bf16[64,3072]{1,0:T(8,128)(2,1)} %copy-done.18, bf16[64,3072]{1,0:T(8,128)(2,1)} %collective-permute-done.4.p3), custom_call_target="tpu_custom_call" | custom-call | flops 1024 | bytes 1024 | tf_op jit(solution)/shard_map/stack/pallas_call | solution.py:103
  28.9 2.4 %collective-permute-start.5 = (bf16[256,2048]{1,0:T(8,128)(2,1)}, bf16[256,2048]{1,0:T(8,128)(2,1)}, u32[]{:S(2)}, u32[]{:S(2)}) collective-permute-start(bf16[256,2048]{1,0:T(8,128)(2,1)} %get-tuple-element.69.p0), channel_id=1, source_target_pairs={{0,24},{1,7},{2,26},{3,1},{4,28},{5,3},{6,30},{7,5},{8,0},{9,15},{... | collective-permute-start | bytes 3145736 | tf_op jit(solution)/shard_map/ppermute | solution.py:74
  33.2 3.6 %multiply_convert_fusion.cot = bf16[1024,1024]{1,0:T(8,128)(2,1)} fusion(bf16[512,1024]{1,0:T(8,128)(2,1)} %collective-permute-done.8, bf16[512,1024]{1,0:T(8,128)(2,1)S(1)} %copy-done.1, f32[1024]{0:T(1024)S(1)} %bitcast.18, pred[]{:T(512)S(6)} %eq.14), kind=kLoop, calls=%fused_computation.3 | loop fusion | flops 12582912 | bytes 4198401 | tf_op jit(solution)/shard_map/convert_element_type | solution.py:693
  36.8 4.8 %convert_multiply_fusion = (f32[1024,1024]{1,0:T(8,128)S(1)}, bf16[1024,1024]{1,0:T(8,128)(2,1)}) fusion(f32[1024]{0:T(1024)S(1)} %add_rsqrt_fusion, bf16[512,1024]{1,0:T(8,128)(2,1)S(1)} %copy-done.2, bf16[512,1024]{1,0:T(8,128)(2,1)S(1)} %collective-permute-done, pred[]{:T(512)S(6)} %eq.14, f32[1024]{0:T(1024)S(1)} %copy-done.20), kind=kLoop, calls=%fused_computation | loop fusion | flops 13631488 | bytes 8396801 | tf_op jit(solution)/shard_map/mul | solution.py:690
  41.6 13.1 %collective-permute-done.5.p1 = bf16[256,2048]{1,0:T(8,128)(2,1)} collective-permute-done((bf16[256,2048]{1,0:T(8,128)(2,1)}, bf16[256,2048]{1,0:T(8,128)(2,1)}, u32[]{:S(2)}, u32[]{:S(2)}) %collective-permute-start.5) | collective-permute-done | bytes 1048608 | tf_op jit(solution)/shard_map/ppermute | solution.py:74
  54.7 3.7 %collective-permute-done.7.p3 = bf16[256,2048]{1,0:T(8,128)(2,1)} collective-permute-done((bf16[256,2048]{1,0:T(8,128)(2,1)}, bf16[256,2048]{1,0:T(8,128)(2,1)}, u32[]{:S(2)}, u32[]{:S(2)}) %collective-permute-start.7) | collective-permute-done | bytes 1048608 | tf_op jit(solution)/shard_map/ppermute | solution.py:74
  59.3 2.1 %collective-permute-start.9 = (bf16[256,1024]{1,0:T(8,128)(2,1)S(1)}, bf16[256,1024]{1,0:T(8,128)(2,1)}, u32[]{:S(2)}, u32[]{:S(2)}) collective-permute-start(bf16[256,1024]{1,0:T(8,128)(2,1)S(1)} %copy-done.6), channel_id=1, source_target_pairs={{0,24},{1,7},{2,26},{3,1},{4,28},{5,3},{6,30},{7,5},{8,0},{9,15},{... | collective-permute-start | bytes 1572872 | tf_op jit(solution)/shard_map/ppermute | solution.py:74
  61.4 12.5 %project.1 = (bf16[1024,2048]{1,0:T(8,128)(2,1)}, bf16[1024,512]{1,0:T(8,128)(2,1)}, bf16[1024,2048]{1,0:T(8,128)(2,1)}) custom-call(s32[4]{0:T(128)} %pad_add_fusion.ids, bf16[1024,1024]{1,0:T(8,128)(2,1)} %get-tuple-element.68.normed.x, f32[1024,128]{1,0:T(8,128)} %get-tuple-element.127.cos, f32[1024,128]{1,0:T(8,128)} %get-tuple-element.128.sin, ...), custom_call_target="tpu_custom_call" | custom-call | flops 1024 | bytes 1024 | tf_op jit(solution)/shard_map/project/pallas_call | solution.py:172
  73.9 8.6 %attend.1 = (bf16[1024,512]{1,0:T(8,128)(2,1)}, bf16[1024,512]{1,0:T(8,128)(2,1)}, f32[8,2,512]{2,1,0:T(2,128)}) custom-call(s32[4]{0:T(128)} %pad_add_fusion.ids, bf16[1024,2048]{1,0:T(8,128)(2,1)} %get-tuple-element.74.qkv, s32[2,1,512]{2,1,0:T(1,128)} %broadcast_in_dim.82.start), custom_call_target="tpu_custom_call" | custom-call | flops 1024 | bytes 1024 | tf_op jit(solution)/shard_map/attend/pallas_call | solution.py:269
  82.5 3.5 %collective-permute-start.13 = (bf16[1024,512]{1,0:T(8,128)(2,1)}, bf16[1024,512]{1,0:T(8,128)(2,1)S(1)}, u32[]{:S(2)}, u32[]{:S(2)}) collective-permute-start(bf16[1024,512]{1,0:T(8,128)(2,1)} %get-tuple-element.84), channel_id=1, source_target_pairs={{0,1},{1,0},{2,3},{3,2},{4,5},{5,4},{6,7},{7,6},{8,9},{9,8},{10,11... | collective-permute-start | bytes 3145736 | tf_op jit(solution)/shard_map/ppermute | solution.py:40
  87.0 5.4 %to_mixed.1 = (bf16[1024,512]{1,0:T(8,128)(2,1)}, bf16[1024,512]{1,0:T(8,128)(2,1)}) custom-call(s32[4]{0:T(128)} %pad_add_fusion.ids, bf16[1024,1024]{1,0:T(8,128)(2,1)} %multiply_convert_fusion.cot, bf16[256,1024]{1,0:T(8,128)(2,1)} %get-tuple-element.76.p0, bf16[256,1024]{1,0:T(8,128)(2,1)} %collective-permute-done.9.p1, bf16[256,1024]{1,0:T(8,128)(2,1)} %copy-done.7, ...), custom_call_target="tpu_custom_call" | custom-call | flops 1024 | bytes 1024 | tf_op jit(solution)/shard_map/to_mixed/pallas_call | solution.py:431
  93.4 5.8 %output_pieces.1 = (bf16[256,1024]{1,0:T(8,128)(2,1)}, bf16[256,1024]{1,0:T(8,128)(2,1)}, bf16[256,1024]{1,0:T(8,128)(2,1)}, bf16[256,1024]{1,0:T(8,128)(2,1)}) custom-call(s32[4]{0:T(128)} %pad_add_fusion.ids, bf16[1024,512]{1,0:T(8,128)(2,1)} %get-tuple-element.83.keep, bf16[1024,512]{1,0:T(8,128)(2,1)} %copy-done.4, ...), custom_call_target="tpu_custom_call" | custom-call | flops 1024 | bytes 1024 | tf_op jit(solution)/shard_map/output_pieces/pallas_call | solution.py:470
  99.2 2.7 %collective-permute-start.15 = (bf16[256,1024]{1,0:T(8,128)(2,1)}, bf16[256,1024]{1,0:T(8,128)(2,1)S(1)}, u32[]{:S(2)}, u32[]{:S(2)}) collective-permute-start(bf16[256,1024]{1,0:T(8,128)(2,1)} %get-tuple-element.87), channel_id=1, source_target_pairs={{0,24},{1,7},{2,26},{3,1},{4,28},{5,3},{6,30},{7,5},{8,0},{9,15},{... | collective-permute-start | bytes 1572872 | tf_op jit(solution)/shard_map/ppermute | solution.py:74
  102.9 18.4 %attend_back.1 = (bf16[1024,2048]{1,0:T(8,128)(2,1)}, f32[1,128]{1,0:T(1,128)}, f32[1,128]{1,0:T(1,128)}) custom-call(s32[4]{0:T(128)} %pad_add_fusion.ids, bf16[1024,2048]{1,0:T(8,128)(2,1)} %get-tuple-element.74.qkv, bf16[1024,512]{1,0:T(8,128)(2,1)} %get-tuple-element.77.dm_a, bf16[1024,512]{1,0:T(8,128)(2,1)} %copy-done.5, ...), custom_call_target="tpu_custom_call" | custom-call | flops 1024 | bytes 1024 | tf_op jit(solution)/shard_map/attend_back/pallas_call | solution.py:383
  121.3 10.2 %weight_pieces.1 = (bf16[256,2176]{1,0:T(8,128)(2,1)}, bf16[256,2176]{1,0:T(8,128)(2,1)}, bf16[256,2176]{1,0:T(8,128)(2,1)}, bf16[256,2176]{1,0:T(8,128)(2,1)}) custom-call(s32[4]{0:T(128)} %pad_add_fusion.ids, bf16[1024,1024]{1,0:T(8,128)(2,1)} %get-tuple-element.68.normed.x, bf16[1024,2048]{1,0:T(8,128)(2,1)} %get-tuple-element.73.w, ...), custom_call_target="tpu_custom_call" | custom-call | flops 1024 | bytes 1024 | tf_op jit(solution)/shard_map/weight_pieces/pallas_call | solution.py:544
  132.2 2.1 %collective-permute-start.19 = (bf16[256,2176]{1,0:T(8,128)(2,1)}, bf16[256,2176]{1,0:T(8,128)(2,1)}, u32[]{:S(2)}, u32[]{:S(2)}) collective-permute-start(bf16[256,2176]{1,0:T(8,128)(2,1)} %get-tuple-element.101), channel_id=1, source_target_pairs={{0,24},{1,7},{2,26},{3,1},{4,28},{5,3},{6,30},{7,5},{8,0},{9,15},{... | collective-permute-start | bytes 3342344 | tf_op jit(solution)/shard_map/ppermute | solution.py:74
  136.0 9.9 %to_normed.1 = (bf16[512,1024]{1,0:T(8,128)(2,1)}, f32[512,1024]{1,0:T(8,128)}) custom-call(s32[4]{0:T(128)} %pad_add_fusion.ids, bf16[1024,2048]{1,0:T(8,128)(2,1)} %get-tuple-element.96.up.du, bf16[1024,2048]{1,0:T(8,128)(2,1)} %get-tuple-element.73.w), custom_call_target="tpu_custom_call" | custom-call | flops 1024 | bytes 1024 | tf_op jit(solution)/shard_map/to_normed/pallas_call | solution.py:579
  145.9 2.2 %collective-permute-start.17 = (bf16[512,1024]{1,0:T(8,128)(2,1)}, bf16[512,1024]{1,0:T(8,128)(2,1)}, u32[]{:S(2)}, u32[]{:S(2)}) collective-permute-start(bf16[512,1024]{1,0:T(8,128)(2,1)} %get-tuple-element.98), channel_id=1, source_target_pairs={{0,1},{1,0},{2,3},{3,2},{4,5},{5,4},{6,7},{7,6},{8,9},{9,8},{10,11... | collective-permute-start | bytes 3145736 | tf_op jit(solution)/shard_map/ppermute | solution.py:40
  148.1 10.9 %collective-permute-done.19.refs_2_ = bf16[256,2176]{1,0:T(8,128)(2,1)} collective-permute-done((bf16[256,2176]{1,0:T(8,128)(2,1)}, bf16[256,2176]{1,0:T(8,128)(2,1)}, u32[]{:S(2)}, u32[]{:S(2)}) %collective-permute-start.19) | collective-permute-done | bytes 1114144 | tf_op jit(solution)/shard_map/ppermute | solution.py:74
  160.0 4.4 %add_split.1 = (bf16[64,3200]{1,0:T(8,128)(2,1)}, bf16[64,3200]{1,0:T(8,128)(2,1)}, bf16[64,3200]{1,0:T(8,128)(2,1)}, bf16[64,3200]{1,0:T(8,128)(2,1)}) custom-call(s32[4]{0:T(128)} %pad_add_fusion.ids, bf16[256,2176]{1,0:T(8,128)(2,1)} %get-tuple-element.99.refs_0_, bf16[256,2176]{1,0:T(8,128)(2,1)} %collective-permute-done.18.refs_1_, ...), custom_call_target="tpu_custom_call" | custom-call | flops 1024 | bytes 1024 | tf_op jit(solution)/shard_map/add_split/pallas_call | solution.py:103
  164.4 2.7 %collective-permute-start.22 = (bf16[64,3200]{1,0:T(8,128)(2,1)}, bf16[64,3200]{1,0:T(8,128)(2,1)S(1)}, u32[]{:S(2)}, u32[]{:S(2)}) collective-permute-start(bf16[64,3200]{1,0:T(8,128)(2,1)} %get-tuple-element.109), channel_id=1, source_target_pairs={{0,6},{1,25},{2,0},{3,27},{4,2},{5,29},{6,4},{7,31},{8,14},{9,1},{... | collective-permute-start | bytes 1228808 | tf_op jit(solution)/shard_map/ppermute | solution.py:74
  169.0 8.4 %collective-permute-done.21.b = bf16[64,3200]{1,0:T(8,128)(2,1)S(1)} collective-permute-done((bf16[64,3200]{1,0:T(8,128)(2,1)}, bf16[64,3200]{1,0:T(8,128)(2,1)S(1)}, u32[]{:S(2)}, u32[]{:S(2)}) %collective-permute-start.21) | collective-permute-done | bytes 409632 | tf_op jit(solution)/shard_map/ppermute | solution.py:74
  178.3 2.3 %share.1 = (bf16[32,4224]{1,0:T(8,128)(2,1)}, bf16[32,2176]{1,0:T(8,128)(2,1)}) custom-call(s32[4]{0:T(128)} %pad_add_fusion.ids, bf16[64,3200]{1,0:T(8,128)(2,1)} %get-tuple-element.107.a, bf16[64,3200]{1,0:T(8,128)(2,1)} %copy-done.13, bf16[64,3200]{1,0:T(8,128)(2,1)} %copy-done.15, bf16[64,3200]{1,0:T(8,128)(2,1)} %collective-permute-done.23.d), custom_call_target="tpu_custom_call" | custom-call | flops 1024 | bytes 1024 | tf_op jit(solution)/shard_map/share/pallas_call | solution.py:103
  180.6 3.1 %collective-permute-start.24 = (bf16[32,2176]{1,0:T(8,128)(2,1)}, bf16[32,2176]{1,0:T(8,128)(2,1)S(1)}, u32[]{:S(2)}, u32[]{:S(2)}) collective-permute-start(bf16[32,2176]{1,0:T(8,128)(2,1)} %get-tuple-element.112), channel_id=1, source_target_pairs={{0,1},{1,0},{2,3},{3,2},{4,5},{5,4},{6,7},{7,6},{8,9},{9,8},{10,11... | collective-permute-start | bytes 417800 | tf_op jit(solution)/shard_map/ppermute | solution.py:40
  185.0 2.8 %collective-permute-start.25 = (bf16[32,6400]{1,0:T(8,128)(2,1)S(1)}, bf16[32,6400]{1,0:T(8,128)(2,1)S(1)}, u32[]{:S(2)}, u32[]{:S(2)}) collective-permute-start(bf16[32,6400]{1,0:T(8,128)(2,1)S(1)} %constant_dynamic-update-slice_fusion.a), channel_id=1, source_target_pairs={{0,64},{32,96},{64,0},{96,32},{1,65},{33,97},{65,1},{97,33},{2,66}... | collective-permute-start | bytes 1228808 | tf_op jit(solution)/shard_map/ppermute | solution.py:36
  188.1 2.4 %collective-permute-start.27 = (bf16[32,6400]{1,0:T(8,128)(2,1)S(1)}, bf16[32,6400]{1,0:T(8,128)(2,1)S(1)}, u32[]{:S(2)}, u32[]{:S(2)}) collective-permute-start(bf16[32,6400]{1,0:T(8,128)(2,1)S(1)} %constant_dynamic-update-slice_fusion.a), channel_id=1, source_target_pairs={{0,96},{32,0},{64,32},{96,64},{1,97},{33,1},{65,33},{97,65},{2,98}... | collective-permute-start | bytes 1228808 | tf_op jit(solution)/shard_map/ppermute | solution.py:36
  190.5 3.0 %add_convert_fusion = bf16[512,1024]{1,0:T(8,128)(2,1)} fusion(bf16[512,1024]{1,0:T(8,128)(2,1)S(1)} %copy-done.1, f32[512,1024]{1,0:T(8,128)S(1)} %copy-done, bf16[512,1024]{1,0:T(8,128)(2,1)} %collective-permute-done.17, f32[512]{0:T(512)S(1)} %bitcast.21, f32[512]{0:T(512)S(1)} %broadcast_multiply_fusion, f32[1024]{0:T(1024)S(1)} %copy-done.20, ...), kind=kLoop, calls=%fused_computation.8 | loop fusion | flops 5767168 | bytes 9447425 | tf_op jit(solution)/shard_map/convert_element_type | solution.py:722
  193.5 3.9 %collective-permute-done.25.b = bf16[32,6400]{1,0:T(8,128)(2,1)S(1)} collective-permute-done((bf16[32,6400]{1,0:T(8,128)(2,1)S(1)}, bf16[32,6400]{1,0:T(8,128)(2,1)S(1)}, u32[]{:S(2)}, u32[]{:S(2)}) %collective-permute-start.25) | collective-permute-done | bytes 409632 | tf_op jit(solution)/shard_map/ppermute | solution.py:36
  197.3 9.4 %collective-permute-done.26.c = bf16[32,6400]{1,0:T(8,128)(2,1)S(1)} collective-permute-done((bf16[32,6400]{1,0:T(8,128)(2,1)S(1)}, bf16[32,6400]{1,0:T(8,128)(2,1)S(1)}, u32[]{:S(2)}, u32[]{:S(2)}) %collective-permute-start.26) | collective-permute-done | bytes 409632 | tf_op jit(solution)/shard_map/ppermute | solution.py:36
  208.3 2.4 %finish.1 = (f32[32,2048]{1,0:T(8,128)}, f32[32,1024]{1,0:T(8,128)}, f32[32,1024]{1,0:T(8,128)}, f32[64,1024]{1,0:T(8,128)}, f32[8,128]{1,0:T(8,128)}, /*index=5*/f32[1,128]{1,0:T(1,128)}, f32[1,128]{1,0:T(1,128)}) custom-call(s32[4]{0:T(128)} %pad_add_fusion.ids, f32[8,128]{1,0:T(8,128)} %bitcast.16, bf16[32,6400]{1,0:T(8,128)(2,1)} %copy-done.3, ...), custom_call_target="tpu_custom_call" | custom-call | flops 1024 | bytes 1024 | tf_op jit(solution)/shard_map/finish/pallas_call | solution.py:646
  (110 shorter events, 33.3 us)
Async XLA Ops:
  4.3 3.0 %collective-permute-start.1 = (bf16[48,2048]{1,0:T(8,128)(2,1)}, bf16[48,2048]{1,0:T(8,128)(2,1)S(1)}, u32[]{:S(2)}, u32[]{:S(2)}) collective-permute-start(bf16[48,2048]{1,0:T(8,128)(2,1)} %get-tuple-element.65), channel_id=1, source_target_pairs={{0,1},{1,0},{2,3},{3,2},{4,5},{5,4},{6,7},{7,6},{8,9},{9,8},{10,11... | collective-permute-start | bytes 589832 | tf_op jit(solution)/shard_map/ppermute | solution.py:40
  5.7 27.4 %collective-permute-start.8 = (bf16[512,1024]{1,0:T(8,128)(2,1)}, bf16[512,1024]{1,0:T(8,128)(2,1)}, u32[]{:S(2)}, u32[]{:S(2)}) collective-permute-start(bf16[512,1024]{1,0:T(8,128)(2,1)} %param.13), channel_id=1, source_target_pairs={{0,1},{1,0},{2,3},{3,2},{4,5},{5,4},{6,7},{7,6},{8,9},{9,8},{10,11... | collective-permute-start | bytes 3145736 | tf_op jit(solution)/shard_map/ppermute | solution.py:40
  5.7 26.7 %collective-permute-start = (bf16[512,1024]{1,0:T(8,128)(2,1)}, bf16[512,1024]{1,0:T(8,128)(2,1)S(1)}, u32[]{:S(2)}, u32[]{:S(2)}) collective-permute-start(bf16[512,1024]{1,0:T(8,128)(2,1)} %param.12), channel_id=1, source_target_pairs={{0,1},{1,0},{2,3},{3,2},{4,5},{5,4},{6,7},{7,6},{8,9},{9,8},{10,11... | collective-permute-start | bytes 3145736 | tf_op jit(solution)/shard_map/ppermute | solution.py:40
  9.8 13.1 %collective-permute-start.2 = (bf16[64,3072]{1,0:T(8,128)(2,1)}, bf16[64,3072]{1,0:T(8,128)(2,1)S(1)}, u32[]{:S(2)}, u32[]{:S(2)}) collective-permute-start(bf16[64,3072]{1,0:T(8,128)(2,1)} %join.1.p0), channel_id=1, source_target_pairs={{0,6},{1,25},{2,0},{3,27},{4,2},{5,29},{6,4},{7,31},{8,14},{9,1},{... | collective-permute-start | bytes 1179656 | tf_op jit(solution)/shard_map/ppermute | solution.py:74
  13.6 9.3 %collective-permute-start.3 = (bf16[64,3072]{1,0:T(8,128)(2,1)}, bf16[64,3072]{1,0:T(8,128)(2,1)S(1)}, u32[]{:S(2)}, u32[]{:S(2)}) collective-permute-start(bf16[64,3072]{1,0:T(8,128)(2,1)} %join.1.p0), channel_id=1, source_target_pairs={{0,4},{1,17},{2,6},{3,19},{4,0},{5,21},{6,2},{7,23},{8,12},{9,25},... | collective-permute-start | bytes 1179656 | tf_op jit(solution)/shard_map/ppermute | solution.py:74
  13.6 12.7 %collective-permute-start.4 = (bf16[64,3072]{1,0:T(8,128)(2,1)}, bf16[64,3072]{1,0:T(8,128)(2,1)}, u32[]{:S(2)}, u32[]{:S(2)}) collective-permute-start(bf16[64,3072]{1,0:T(8,128)(2,1)} %join.1.p0), channel_id=1, source_target_pairs={{0,2},{1,9},{2,4},{3,11},{4,6},{5,13},{6,0},{7,15},{8,10},{9,17},{... | collective-permute-start | bytes 1179656 | tf_op jit(solution)/shard_map/ppermute | solution.py:74
  19.7 12.7 %copy-start.2 = (bf16[512,1024]{1,0:T(8,128)(2,1)S(1)}, bf16[512,1024]{1,0:T(8,128)(2,1)}, u32[]{:S(2)}) copy-start(bf16[512,1024]{1,0:T(8,128)(2,1)} %param.12) | copy-start | bytes 3145732
  21.0 12.2 %copy-start.1 = (bf16[512,1024]{1,0:T(8,128)(2,1)S(1)}, bf16[512,1024]{1,0:T(8,128)(2,1)}, u32[]{:S(2)}) copy-start(bf16[512,1024]{1,0:T(8,128)(2,1)} %param.13) | copy-start | bytes 3145732
  28.9 25.8 %collective-permute-start.5 = (bf16[256,2048]{1,0:T(8,128)(2,1)}, bf16[256,2048]{1,0:T(8,128)(2,1)}, u32[]{:S(2)}, u32[]{:S(2)}) collective-permute-start(bf16[256,2048]{1,0:T(8,128)(2,1)} %get-tuple-element.69.p0), channel_id=1, source_target_pairs={{0,24},{1,7},{2,26},{3,1},{4,28},{5,3},{6,30},{7,5},{8,0},{9,15},{... | collective-permute-start | bytes 3145736 | tf_op jit(solution)/shard_map/ppermute | solution.py:74
  31.4 23.3 %collective-permute-start.6 = (bf16[256,2048]{1,0:T(8,128)(2,1)}, bf16[256,2048]{1,0:T(8,128)(2,1)}, u32[]{:S(2)}, u32[]{:S(2)}) collective-permute-start(bf16[256,2048]{1,0:T(8,128)(2,1)} %get-tuple-element.69.p0), channel_id=1, source_target_pairs={{0,16},{1,5},{2,18},{3,7},{4,20},{5,1},{6,22},{7,3},{8,24},{9,13},... | collective-permute-start | bytes 3145736 | tf_op jit(solution)/shard_map/ppermute | solution.py:74
  31.7 26.6 %collective-permute-start.7 = (bf16[256,2048]{1,0:T(8,128)(2,1)}, bf16[256,2048]{1,0:T(8,128)(2,1)}, u32[]{:S(2)}, u32[]{:S(2)}) collective-permute-start(bf16[256,2048]{1,0:T(8,128)(2,1)} %get-tuple-element.69.p0), channel_id=1, source_target_pairs={{0,8},{1,3},{2,10},{3,5},{4,12},{5,7},{6,14},{7,1},{8,16},{9,11},{... | collective-permute-start | bytes 3145736 | tf_op jit(solution)/shard_map/ppermute | solution.py:74
  36.8 21.6 %copy-start.6 = (bf16[256,1024]{1,0:T(8,128)(2,1)S(1)}, bf16[256,1024]{1,0:T(8,128)(2,1)}, u32[]{:S(2)}) copy-start(bf16[256,1024]{1,0:T(8,128)(2,1)} %get-tuple-element.76.p0) | copy-start | bytes 1572868
  58.4 27.6 %collective-permute-start.10 = (bf16[256,1024]{1,0:T(8,128)(2,1)S(1)}, bf16[256,1024]{1,0:T(8,128)(2,1)S(1)}, u32[]{:S(2)}, u32[]{:S(2)}) collective-permute-start(bf16[256,1024]{1,0:T(8,128)(2,1)S(1)} %copy-done.6), channel_id=1, source_target_pairs={{0,16},{1,5},{2,18},{3,7},{4,20},{5,1},{6,22},{7,3},{8,24},{9,13},... | collective-permute-start | bytes 1572872 | tf_op jit(solution)/shard_map/ppermute | solution.py:74
  58.7 27.3 %collective-permute-start.11 = (bf16[256,1024]{1,0:T(8,128)(2,1)S(1)}, bf16[256,1024]{1,0:T(8,128)(2,1)S(1)}, u32[]{:S(2)}, u32[]{:S(2)}) collective-permute-start(bf16[256,1024]{1,0:T(8,128)(2,1)S(1)} %copy-done.6), channel_id=1, source_target_pairs={{0,8},{1,3},{2,10},{3,5},{4,12},{5,7},{6,14},{7,1},{8,16},{9,11},{... | collective-permute-start | bytes 1572872 | tf_op jit(solution)/shard_map/ppermute | solution.py:74
  59.3 26.7 %collective-permute-start.9 = (bf16[256,1024]{1,0:T(8,128)(2,1)S(1)}, bf16[256,1024]{1,0:T(8,128)(2,1)}, u32[]{:S(2)}, u32[]{:S(2)}) collective-permute-start(bf16[256,1024]{1,0:T(8,128)(2,1)S(1)} %copy-done.6), channel_id=1, source_target_pairs={{0,24},{1,7},{2,26},{3,1},{4,28},{5,3},{6,30},{7,5},{8,0},{9,15},{... | collective-permute-start | bytes 1572872 | tf_op jit(solution)/shard_map/ppermute | solution.py:74
  82.5 9.9 %collective-permute-start.13 = (bf16[1024,512]{1,0:T(8,128)(2,1)}, bf16[1024,512]{1,0:T(8,128)(2,1)S(1)}, u32[]{:S(2)}, u32[]{:S(2)}) collective-permute-start(bf16[1024,512]{1,0:T(8,128)(2,1)} %get-tuple-element.84), channel_id=1, source_target_pairs={{0,1},{1,0},{2,3},{3,2},{4,5},{5,4},{6,7},{7,6},{8,9},{9,8},{10,11... | collective-permute-start | bytes 3145736 | tf_op jit(solution)/shard_map/ppermute | solution.py:40
  92.4 9.5 %collective-permute-start.12 = (bf16[1024,512]{1,0:T(8,128)(2,1)}, bf16[1024,512]{1,0:T(8,128)(2,1)S(1)}, u32[]{:S(2)}, u32[]{:S(2)}) collective-permute-start(bf16[1024,512]{1,0:T(8,128)(2,1)} %get-tuple-element.78), channel_id=1, source_target_pairs={{0,1},{1,0},{2,3},{3,2},{4,5},{5,4},{6,7},{7,6},{8,9},{9,8},{10,11... | collective-permute-start | bytes 3145736 | tf_op jit(solution)/shard_map/ppermute | solution.py:40
  99.2 22.0 %collective-permute-start.14 = (bf16[256,1024]{1,0:T(8,128)(2,1)}, bf16[256,1024]{1,0:T(8,128)(2,1)S(1)}, u32[]{:S(2)}, u32[]{:S(2)}) collective-permute-start(bf16[256,1024]{1,0:T(8,128)(2,1)} %get-tuple-element.86), channel_id=1, source_target_pairs={{0,8},{1,3},{2,10},{3,5},{4,12},{5,7},{6,14},{7,1},{8,16},{9,11},{... | collective-permute-start | bytes 1572872 | tf_op jit(solution)/shard_map/ppermute | solution.py:74
  99.2 22.1 %collective-permute-start.15 = (bf16[256,1024]{1,0:T(8,128)(2,1)}, bf16[256,1024]{1,0:T(8,128)(2,1)S(1)}, u32[]{:S(2)}, u32[]{:S(2)}) collective-permute-start(bf16[256,1024]{1,0:T(8,128)(2,1)} %get-tuple-element.87), channel_id=1, source_target_pairs={{0,24},{1,7},{2,26},{3,1},{4,28},{5,3},{6,30},{7,5},{8,0},{9,15},{... | collective-permute-start | bytes 1572872 | tf_op jit(solution)/shard_map/ppermute | solution.py:74
  101.9 19.4 %collective-permute-start.16 = (bf16[256,1024]{1,0:T(8,128)(2,1)}, bf16[256,1024]{1,0:T(8,128)(2,1)S(1)}, u32[]{:S(2)}, u32[]{:S(2)}) collective-permute-start(bf16[256,1024]{1,0:T(8,128)(2,1)} %get-tuple-element.88), channel_id=1, source_target_pairs={{0,16},{1,5},{2,18},{3,7},{4,20},{5,1},{6,22},{7,3},{8,24},{9,13},... | collective-permute-start | bytes 1572872 | tf_op jit(solution)/shard_map/ppermute | solution.py:74
  131.5 16.6 %collective-permute-start.18 = (bf16[256,2176]{1,0:T(8,128)(2,1)}, bf16[256,2176]{1,0:T(8,128)(2,1)}, u32[]{:S(2)}, u32[]{:S(2)}) collective-permute-start(bf16[256,2176]{1,0:T(8,128)(2,1)} %get-tuple-element.100), channel_id=1, source_target_pairs={{0,8},{1,3},{2,10},{3,5},{4,12},{5,7},{6,14},{7,1},{8,16},{9,11},{... | collective-permute-start | bytes 3342344 | tf_op jit(solution)/shard_map/ppermute | solution.py:74
  132.2 26.8 %collective-permute-start.19 = (bf16[256,2176]{1,0:T(8,128)(2,1)}, bf16[256,2176]{1,0:T(8,128)(2,1)}, u32[]{:S(2)}, u32[]{:S(2)}) collective-permute-start(bf16[256,2176]{1,0:T(8,128)(2,1)} %get-tuple-element.101), channel_id=1, source_target_pairs={{0,24},{1,7},{2,26},{3,1},{4,28},{5,3},{6,30},{7,5},{8,0},{9,15},{... | collective-permute-start | bytes 3342344 | tf_op jit(solution)/shard_map/ppermute | solution.py:74
  134.3 25.7 %collective-permute-start.20 = (bf16[256,2176]{1,0:T(8,128)(2,1)}, bf16[256,2176]{1,0:T(8,128)(2,1)}, u32[]{:S(2)}, u32[]{:S(2)}) collective-permute-start(bf16[256,2176]{1,0:T(8,128)(2,1)} %get-tuple-element.102), channel_id=1, source_target_pairs={{0,16},{1,5},{2,18},{3,7},{4,20},{5,1},{6,22},{7,3},{8,24},{9,13},... | collective-permute-start | bytes 3342344 | tf_op jit(solution)/shard_map/ppermute | solution.py:74
  145.9 21.4 %collective-permute-start.17 = (bf16[512,1024]{1,0:T(8,128)(2,1)}, bf16[512,1024]{1,0:T(8,128)(2,1)}, u32[]{:S(2)}, u32[]{:S(2)}) collective-permute-start(bf16[512,1024]{1,0:T(8,128)(2,1)} %get-tuple-element.98), channel_id=1, source_target_pairs={{0,1},{1,0},{2,3},{3,2},{4,5},{5,4},{6,7},{7,6},{8,9},{9,8},{10,11... | collective-permute-start | bytes 3145736 | tf_op jit(solution)/shard_map/ppermute | solution.py:40
  148.1 19.2 %copy-start = (f32[512,1024]{1,0:T(8,128)S(1)}, f32[512,1024]{1,0:T(8,128)}, u32[]{:S(2)}) copy-start(f32[512,1024]{1,0:T(8,128)} %get-tuple-element.97) | copy-start | bytes 6291460
  164.4 13.0 %collective-permute-start.21 = (bf16[64,3200]{1,0:T(8,128)(2,1)}, bf16[64,3200]{1,0:T(8,128)(2,1)S(1)}, u32[]{:S(2)}, u32[]{:S(2)}) collective-permute-start(bf16[64,3200]{1,0:T(8,128)(2,1)} %get-tuple-element.108), channel_id=1, source_target_pairs={{0,2},{1,9},{2,4},{3,11},{4,6},{5,13},{6,0},{7,15},{8,10},{9,17},{... | collective-permute-start | bytes 1228808 | tf_op jit(solution)/shard_map/ppermute | solution.py:74
  164.4 13.0 %collective-permute-start.22 = (bf16[64,3200]{1,0:T(8,128)(2,1)}, bf16[64,3200]{1,0:T(8,128)(2,1)S(1)}, u32[]{:S(2)}, u32[]{:S(2)}) collective-permute-start(bf16[64,3200]{1,0:T(8,128)(2,1)} %get-tuple-element.109), channel_id=1, source_target_pairs={{0,6},{1,25},{2,0},{3,27},{4,2},{5,29},{6,4},{7,31},{8,14},{9,1},{... | collective-permute-start | bytes 1228808 | tf_op jit(solution)/shard_map/ppermute | solution.py:74
  167.1 10.3 %collective-permute-start.23 = (bf16[64,3200]{1,0:T(8,128)(2,1)}, bf16[64,3200]{1,0:T(8,128)(2,1)}, u32[]{:S(2)}, u32[]{:S(2)}) collective-permute-start(bf16[64,3200]{1,0:T(8,128)(2,1)} %get-tuple-element.110), channel_id=1, source_target_pairs={{0,4},{1,17},{2,6},{3,19},{4,0},{5,21},{6,2},{7,23},{8,12},{9,25},... | collective-permute-start | bytes 1228808 | tf_op jit(solution)/shard_map/ppermute | solution.py:74
  180.6 4.3 %collective-permute-start.24 = (bf16[32,2176]{1,0:T(8,128)(2,1)}, bf16[32,2176]{1,0:T(8,128)(2,1)S(1)}, u32[]{:S(2)}, u32[]{:S(2)}) collective-permute-start(bf16[32,2176]{1,0:T(8,128)(2,1)} %get-tuple-element.112), channel_id=1, source_target_pairs={{0,1},{1,0},{2,3},{3,2},{4,5},{5,4},{6,7},{7,6},{8,9},{9,8},{10,11... | collective-permute-start | bytes 417800 | tf_op jit(solution)/shard_map/ppermute | solution.py:40
  185.0 12.3 %collective-permute-start.25 = (bf16[32,6400]{1,0:T(8,128)(2,1)S(1)}, bf16[32,6400]{1,0:T(8,128)(2,1)S(1)}, u32[]{:S(2)}, u32[]{:S(2)}) collective-permute-start(bf16[32,6400]{1,0:T(8,128)(2,1)S(1)} %constant_dynamic-update-slice_fusion.a), channel_id=1, source_target_pairs={{0,64},{32,96},{64,0},{96,32},{1,65},{33,97},{65,1},{97,33},{2,66}... | collective-permute-start | bytes 1228808 | tf_op jit(solution)/shard_map/ppermute | solution.py:36
  187.8 18.9 %collective-permute-start.26 = (bf16[32,6400]{1,0:T(8,128)(2,1)S(1)}, bf16[32,6400]{1,0:T(8,128)(2,1)S(1)}, u32[]{:S(2)}, u32[]{:S(2)}) collective-permute-start(bf16[32,6400]{1,0:T(8,128)(2,1)S(1)} %constant_dynamic-update-slice_fusion.a), channel_id=1, source_target_pairs={{0,32},{32,64},{64,96},{96,0},{1,33},{33,65},{65,97},{97,1},{2,34}... | collective-permute-start | bytes 1228808 | tf_op jit(solution)/shard_map/ppermute | solution.py:36
  188.1 18.6 %collective-permute-start.27 = (bf16[32,6400]{1,0:T(8,128)(2,1)S(1)}, bf16[32,6400]{1,0:T(8,128)(2,1)S(1)}, u32[]{:S(2)}, u32[]{:S(2)}) collective-permute-start(bf16[32,6400]{1,0:T(8,128)(2,1)S(1)} %constant_dynamic-update-slice_fusion.a), channel_id=1, source_target_pairs={{0,96},{32,0},{64,32},{96,64},{1,97},{33,1},{65,33},{97,65},{2,98}... | collective-permute-start | bytes 1228808 | tf_op jit(solution)/shard_map/ppermute | solution.py:36
  (17 other events, 68.2 us)

commit v2 on v1

--- a/solution.py
+++ b/solution.py
@@ -19,7 +19,7 @@
 LOG2E = 1.4426950408889634
 SCALE = 1.0 / math.sqrt(HD)
 ALL = ("dp", "z", "y", "core")
-VMEM_LIMIT = 56 * 1024 * 1024
+MIB = 1024 * 1024
 BF = jnp.bfloat16
 F32 = jnp.float32
 
@@ -27,8 +27,8 @@
 COST = pl.CostEstimate(flops=1024, bytes_accessed=1024, transcendentals=0)
 
 
-def params(**kw):
-    return pltpu.CompilerParams(vmem_limit_bytes=VMEM_LIMIT, **kw)
+def params(mib=28):
+    return pltpu.CompilerParams(vmem_limit_bytes=mib * MIB)
 
 
 def shift(x, axis, by):
@@ -279,19 +279,22 @@
     )(ids, qkv, start)
 
 
-def backward_kernel(
-    ids, qkv, dm_a, dm_b, lse, factors, cos, sin, qg, kg, start, du, gq_out, gk_out, bias, low, high, dms, scores, dprobs, probs, dscores
+HEAD_STEPS = 4 // PER
+BACK_STEPS = 2 * HEAD_STEPS
+
+
+def attention_step(
+    ids, qkv, dm_a, dm_b, lse, factors, cos, sin, qg, kg, start, du, gain, du_all, bias, low, high, dms, scores, dprobs, probs, dscores
 ):
-    first = (pl.program_id(0) == 0) & (pl.program_id(1) == 0)
-
-    @pl.when(first)
-    def _():
-        gq_out[...] = jnp.zeros_like(gq_out)
-        gk_out[...] = jnp.zeros_like(gk_out)
+    step = pl.program_id(0)
+
+    @pl.when(step == 0)
+    def _():
+        gain[...] = jnp.zeros_like(gain)
         probs[...] = jnp.zeros_like(probs)
         dscores[...] = jnp.zeros_like(dscores)
 
-    @pl.when(pl.program_id(1) == 0)
+    @pl.when(lax.rem(step, HEAD_STEPS) == 0)
     def _():
         fill_bias(start, bias)
 
@@ -307,7 +310,7 @@
 
     c, sn = cos[...], sin[...]
 
-    def unturn(grad, turned, at, gain):
+    def unturn(grad, turned, at, g_head):
         g = grad * c - pltpu.roll(grad, 64, 1) * sn
         turned = turned.astype(F32)
         gained = turned * c - pltpu.roll(turned, 64, 1) * sn
@@ -316,7 +319,7 @@
         lanes = lax.broadcasted_iota(jnp.int32, (HD, HD), 0) % 8
         pick = jnp.where((lanes == at % 4) | (lanes == at % 4 + 4), F32(1.0), F32(0.0)).astype(BF)
         factor = jnp.dot(factors[:, group], pick, preferred_element_type=F32)
-        back = factor * (g * gain - gained * (1.0 / gain) * lane_mean(product))
+        back = factor * (g * g_head - gained * (1.0 / g_head) * lane_mean(product))
         return back.astype(BF), jnp.sum(product, axis=0, keepdims=True)
 
     lane = lax.broadcasted_iota(jnp.int32, (T, HD), 1)
@@ -365,46 +368,133 @@
             du[:, k], more = unturn(jnp.concatenate(dk, axis=0) * F32(SCALE), qkv[:, k], 4 * (n // 2) + 2, kg[...])
             gk = gk + more
             du[:, columns(n, "v")] = jnp.concatenate(dv, axis=0).astype(BF)
-    gq_out[...] += gq / qg[...]
-    gk_out[...] += gk / kg[...]
-
-
-def attend_back(ids, qkv, dm_a, dm_b, lse, factors, cos, sin, qg, kg, start):
-    rows = qkv.shape[0] // T
-    heads = qkv.shape[1] // GROUP
-    steps = heads // PER
+    gain[8:9, :] += gq / qg[...]
+    gain[9:10, :] += gk / kg[...]
+    rows = pl.ds(pl.multiple_of(step // HEAD_STEPS * T, T), T)
+    cols = pl.ds(pl.multiple_of(lax.rem(step, HEAD_STEPS) * PER * GROUP, PER * GROUP), PER * GROUP)
+    du_all[rows, cols] = du[...]
+
+
+def pieces_step(ids, h, outs, x, w, du_all, gain, last, res, left):
+    def departures(h):
+        slot = lax.rem(h, 2)
+        cols = pl.ds(pl.multiple_of(h * GROUP, GROUP), GROUP)
+        return [
+            pltpu.make_async_copy(res.at[slot, row_of(ids, r, s), :], out.at[64 * s : 64 * s + 64, cols], left.at[slot])
+            for r, out in enumerate(outs)
+            for s in range(4)
+        ]
+
+    @pl.when(h >= 2)
+    def _():
+        for copy in departures(h - 2):
+            copy.wait()
+
+    cols = pl.ds(pl.multiple_of(h * GROUP, GROUP), GROUP)
+    every = dot_tn(x[...], du_all[:, cols])
+    for i in range(4):
+        block = slice(256 * i, 256 * (i + 1))
+        got = every[block, :]
+        res[lax.rem(h, 2), block, :] = got.astype(BF)
+        product = got * w[block, cols].astype(F32)
+        dots = product[:, :HD]
+        for j in range(1, GROUP // HD):
+            dots = dots + product[:, j * HD : (j + 1) * HD]
+        dots = jnp.sum(dots.T, axis=0, keepdims=True)
+        gain[2 * i : 2 * i + 1, :] += dots[:, :HD]
+        gain[2 * i + 1 : 2 * i + 2, :] += dots[:, HD:]
+    for copy in departures(h):
+        copy.start()
+
+    @pl.when(h == 3)
+    def _():
+        last[...] = jnp.zeros_like(last)
+        last[0:16, :] = gain[...].astype(BF)
+        extra = [pltpu.make_async_copy(last, out.at[:, WIDTH:], left.at[2]) for out in outs]
+        for copy in extra:
+            copy.start()
+        for copy in departures(h - 1) + departures(h) + extra:
+            copy.wait()
+
+
+def backward_kernel(
+    ids, qkv, dm_a, dm_b, lse, factors, cos, sin, qg, kg, start, x_in, w_in, du, o0, o1, o2, o3, *scratch
+):
+    gain, last, res, left, du_all, x, w, came = scratch[:8]
+    step = pl.program_id(0)
+    arrivals = [pltpu.make_async_copy(x_in, x, came.at[0]), pltpu.make_async_copy(w_in, w, came.at[1])]
+
+    @pl.when(step == 0)
+    def _():
+        for copy in arrivals:
+            copy.start()
+
+    @pl.when(step < BACK_STEPS)
+    def _():
+        attention_step(ids, qkv, dm_a, dm_b, lse, factors, cos, sin, qg, kg, start, du, gain, du_all, *scratch[8:])
+
+    @pl.when(step == BACK_STEPS)
+    def _():
+        for copy in arrivals:
+            copy.wait()
+
+    @pl.when(step >= BACK_STEPS)
+    def _():
+        pieces_step(ids, step - BACK_STEPS, (o0, o1, o2, o3), x, w, du_all, gain, last, res, left)
+
+
+def attend_back(ids, qkv, dm_a, dm_b, lse, factors, cos, sin, qg, kg, start, x, w):
+    rows = qkv.shape[0]
+
+    def at(i):
+        i = jnp.minimum(i, BACK_STEPS - 1)
+        return i // HEAD_STEPS, lax.rem(i, HEAD_STEPS)
 
     def tile(cols):
-        return pl.BlockSpec((T, PER * cols), lambda r, h: (r, h))
-
-    by_row = pl.BlockSpec((T, HD), lambda r, h: (r, 0))
-    gain = pl.BlockSpec((1, HD), lambda r, h: (0, 0))
-    gain_shape = jax.ShapeDtypeStruct((1, HD), F32)
+        return pl.BlockSpec((T, PER * cols), at)
+
+    by_row = pl.BlockSpec((T, HD), lambda i: (at(i)[0], 0))
+    whole = pl.BlockSpec((1, HD), lambda i: (0, 0))
+    piece = jax.ShapeDtypeStruct((256, WIDE), BF)
     return pl.pallas_call(
         backward_kernel,
-        grid=(rows, steps),
+        grid=(BACK_STEPS + 4,),
         in_specs=[
             SMEM,
             tile(GROUP),
             tile(HD),
             tile(HD),
-            pl.BlockSpec((PER, 2, T), lambda r, h: (r * steps + h, 0, 0)),
+            pl.BlockSpec((PER, 2, T), lambda i: (jnp.minimum(i, BACK_STEPS - 1), 0, 0)),
             tile(HD),
             by_row,
             by_row,
-            gain,
-            gain,
-            pl.BlockSpec((1, 1, T), lambda r, h: (r, 0, 0)),
+            whole,
+            whole,
+            pl.BlockSpec((1, 1, T), lambda i: (at(i)[0], 0, 0)),
+            ANY,
+            ANY,
         ],
-        out_specs=[tile(GROUP), gain, gain],
-        out_shape=[jax.ShapeDtypeStruct((rows * T, heads * GROUP), BF), gain_shape, gain_shape],
-        scratch_shapes=[pltpu.VMEM((T, T), F32), pltpu.VMEM((T, PER * HD), F32), pltpu.VMEM((T, PER * HD), F32)]
-        + [pltpu.VMEM((2 * PER, T, HD), BF)]
+        out_specs=[tile(GROUP)] + [ANY] * 4,
+        out_shape=[jax.ShapeDtypeStruct((rows, WIDTH), BF)] + [piece] * 4,
+        scratch_shapes=[
+            pltpu.VMEM((16, HD), F32),
+            pltpu.VMEM((256, HD), BF),
+            pltpu.VMEM((2, D, GROUP), BF),
+            pltpu.SemaphoreType.DMA((3,)),
+            pltpu.VMEM((rows, WIDTH), BF),
+            pltpu.VMEM(x.shape, BF),
+            pltpu.VMEM(w.shape, BF),
+            pltpu.SemaphoreType.DMA((2,)),
+            pltpu.VMEM((T, T), F32),
+            pltpu.VMEM((T, PER * HD), F32),
+            pltpu.VMEM((T, PER * HD), F32),
+            pltpu.VMEM((2 * PER, T, HD), BF),
+        ]
         + [pltpu.VMEM((2 * PER, T, T), kind) for kind in (F32, F32, BF, BF)],
-        compiler_params=params(),
+        compiler_params=params(48),
         cost_estimate=COST,
         name="attend_back",
-    )(ids, qkv, dm_a, dm_b, lse, factors, cos, sin, qg, kg, start)
+    )(ids, qkv, dm_a, dm_b, lse, factors, cos, sin, qg, kg, start, x, w)
 
 
 def to_mixed_kernel(ids, cot, p0, p1, p2, p3, keep, send, wo):
@@ -478,85 +568,6 @@
         cost_estimate=COST,
         name="output_pieces",
     )(ids, keep, got, cot)
-
-
-def pieces_kernel(ids, x, w, up, gq, gk, o0, o1, o2, o3, gain, last, res, left):
-    h = pl.program_id(0)
-    steps = pl.num_programs(0)
-    outs = (o0, o1, o2, o3)
-
-    def departures(h):
-        slot = lax.rem(h, 2)
-        cols = pl.ds(pl.multiple_of(h * GROUP, GROUP), GROUP)
-        return [
-            pltpu.make_async_copy(res.at[slot, row_of(ids, r, s), :], out.at[64 * s : 64 * s + 64, cols], left.at[slot])
-            for r, out in enumerate(outs)
-            for s in range(4)
-        ]
-
-    @pl.when(h == 0)
-    def _():
-        gain[...] = jnp.zeros_like(gain)
-        last[...] = jnp.zeros_like(last)
-
-    @pl.when(h >= 2)
-    def _():
-        for copy in departures(h - 2):
-            copy.wait()
-
-    every = dot_tn(x[...], up[...])
-    for i in range(4):
-        block = slice(256 * i, 256 * (i + 1))
-        got = every[block, :]
-        res[lax.rem(h, 2), block, :] = got.astype(BF)
-        product = got * w[block, :].astype(F32)
-        dots = product[:, :HD]
-        for j in range(1, GROUP // HD):
-            dots = dots + product[:, j * HD : (j + 1) * HD]
-        dots = jnp.sum(dots.T, axis=0, keepdims=True)
-        gain[2 * i : 2 * i + 1, :] += dots[:, :HD]
-        gain[2 * i + 1 : 2 * i + 2, :] += dots[:, HD:]
-    for copy in departures(h):
-        copy.start()
-
-    @pl.when(h == steps - 1)
-    def _():
-        gain[8:9, :] = gq[...]
-        gain[9:10, :] = gk[...]
-        last[0:16, :] = gain[...].astype(BF)
-        extra = [pltpu.make_async_copy(last, out.at[:, WIDTH:], left.at[2]) for out in outs]
-        for copy in extra:
-            copy.start()
-        for copy in departures(h - 1) + departures(h) + extra:
-            copy.wait()
-
-
-def weight_pieces(ids, x, w, up, gq, gk):
-    rows = x.shape[0]
-    piece = (256, WIDTH + HD)
-
-    def whole(shape):
-        return pl.BlockSpec(shape, lambda h: (0, 0))
-
-    def by_head(rows):
-        return pl.BlockSpec((rows, GROUP), lambda h: (0, h))
-
-    return pl.pallas_call(
-        pieces_kernel,
-        grid=(4,),
-        in_specs=[SMEM, whole(x.shape), by_head(D), by_head(rows), whole((1, HD)), whole((1, HD))],
-        out_specs=[ANY] * 4,
-        out_shape=[jax.ShapeDtypeStruct(piece, BF)] * 4,
-        scratch_shapes=[
-            pltpu.VMEM((16, HD), F32),
-            pltpu.VMEM((256, HD), BF),
-            pltpu.VMEM((2, D, GROUP), BF),
-            pltpu.SemaphoreType.DMA((3,)),
-        ],
-        compiler_params=params(),
-        cost_estimate=COST,
-        name="weight_pieces",
-    )(ids, x, w, up, gq, gk)
 
 
 def to_normed_kernel(ids, du, w, theirs, own):
@@ -699,10 +710,8 @@
     dm_keep, dm_send = to_mixed(ids, cotw, wo_parts)
     dm_got = swap(dm_send)
     sum_o = send_line(output_pieces(ids, keep, got, cotw), False)
-    du, gq, gk = attend_back(ids, qkv, dm_keep, dm_got, lse, factors, cos, sin, qg, kg, start)
-    du, sum_o = lax.optimization_barrier((du, sum_o))
-    pieces = weight_pieces(ids, normed, w, du, gq, gk)
-    pieces, du = lax.optimization_barrier((pieces, du))
+    du, *pieces = attend_back(ids, qkv, dm_keep, dm_got, lse, factors, cos, sin, qg, kg, start, normed, w)
+    pieces, du, sum_o = lax.optimization_barrier((pieces, du, sum_o))
     total = send_line(pieces, False)
     theirs, back = to_normed(ids, du, w)
     halves = simple(add_split_kernel, "add_split", [(64, WIDE + D)] * 4, ids, *total, *sum_o)

time: 211 us -> 190 us (0.900)
  Pallas kernels: 86.1 us -> 63.5 us
  waiting for transfers between devices: 56.9 us -> 63.2 us
  other arithmetic: 21.2 us -> 15.9 us
    pallas_call x5, Pallas kernels: 12.9 us -> 3.94 us  [simple(): pl.pallas_call(kernel, in_specs=[SMEM] + [VM] * (len(args) - 1), out_spec...]
    ppermute x18, waiting for transfers between devices: 42.4 us -> 47.2 us  [cross(): return lax.ppermute(x, ('z', 'y', 'core'), pairs)]
    pallas_call x1, Pallas kernels: 9.87 us -> 5.96 us  [to_normed(): pl.pallas_call(to_normed_kernel, grid_spec=pltpu.PrefetchScalarGridSpec(n...]
    pallas_call x2 -> x1, Pallas kernels: 28.6 us -> 27.1 us  [attend_back(): pl.pallas_call(backward_kernel, grid=(BACK_STEPS + 4,), in_specs=[SMEM, t...]
    unnamed x45 -> x33, local copies, waits for them, and re-layouts: 7.02 us -> 7.77 us
  transfers between devices with their start and end apart: 28 -> 28, of which waited for: 11 -> 12; matrix products, arithmetic and copies ran while one was open for 10% -> 8% of each run, Pallas kernels for 33% -> 32%
where the time goes in v2:
time: 190 us; the launch traced here: 189 us
  Pallas kernels  63.5 us (33%)
  waiting for transfers between devices  63.2 us (33%)
  starting transfers between devices  38 us (20%)
  other arithmetic  15.9 us (8%)
  local copies, waits for them, and re-layouts  7.8 us (4%)
    ppermute x18, waiting for transfers between devices, cross(): return lax.ppermute(x, ('z', 'y', 'core'), pairs)  47.2 us
    pallas_call x1, Pallas kernels, attend_back(): pl.pallas_call(backward_kernel, grid=(BACK_STEPS + 4,), in_specs=[SMEM, t...  27.1 us
    ppermute x18, starting transfers between devices, cross(): return lax.ppermute(x, ('z', 'y', 'core'), pairs)  21.4 us
    ppermute x3, waiting for transfers between devices, shift(): return lax.ppermute(x, axis, [(i, (i + by) % n) for i in range(n)])  14.5 us
    ppermute x7, starting transfers between devices, swap(): return lax.ppermute(x, 'core', [(0, 1), (1, 0)])  11.2 us
    pallas_call x1, Pallas kernels, project(): pl.pallas_call(project_kernel, grid=(4,), in_specs=[SMEM, whole((rows, D)...  10.5 us
    unnamed x33, local copies, waits for them, and re-layouts  7.77 us
    pallas_call x1, Pallas kernels, attend(): pl.pallas_call(forward_kernel, grid=(rows, steps), in_specs=[SMEM, pl.Blo...  7.28 us
  transfers between devices with their start and end apart: 28, of which 12 were waited for; matrix products, arithmetic and copies ran while one was open for 8% of the time, Pallas kernels for 32%

profile of v2, /device:TPU:1, one launch (start us, length us, event | category | flops | bytes accessed | tf_op | source)
XLA Modules:
  0.0 189.3 jit_solution(8364372947968452729)
XLA Ops:
  8.7 3.9 %collective-permute-start.2 = (bf16[64,3072]{1,0:T(8,128)(2,1)S(1)}, bf16[64,3072]{1,0:T(8,128)(2,1)S(1)}, u32[]{:S(2)}, u32[]{:S(2)}) collective-permute-start(bf16[64,3072]{1,0:T(8,128)(2,1)S(1)} %join.1.p0), channel_id=1, source_target_pairs={{0,6},{1,25},{2,0},{3,27},{4,2},{5,29},{6,4},{7,31},{8,14},{9,1},{... | collective-permute-start | bytes 1179656 | tf_op jit(solution)/shard_map/ppermute | solution.py:74
  15.5 1.9 %fusion.1 = (f32[1024,64]{1,0:T(8,128)S(1)}, f32[1024,64]{1,0:T(8,128)S(1)}, f32[1024,64]{1,0:T(8,128)S(1)}) fusion(f32[64]{0:T(128)S(1)} %multiply_power_fusion, f32[1024]{0:T(1024)S(1)} %bitcast.23), kind=kLoop, calls=%fused_computation.15 | loop fusion | flops 131072 | bytes 790784 | tf_op jit(solution)/shard_map/neg | solution.py:697
  17.8 3.8 %collective-permute-done.2.p1 = bf16[64,3072]{1,0:T(8,128)(2,1)S(1)} collective-permute-done((bf16[64,3072]{1,0:T(8,128)(2,1)S(1)}, bf16[64,3072]{1,0:T(8,128)(2,1)S(1)}, u32[]{:S(2)}, u32[]{:S(2)}) %collective-permute-start.2) | collective-permute-done | bytes 393248 | tf_op jit(solution)/shard_map/ppermute | solution.py:74
  21.6 3.4 %collective-permute-done.4.p3 = bf16[64,3072]{1,0:T(8,128)(2,1)S(1)} collective-permute-done((bf16[64,3072]{1,0:T(8,128)(2,1)S(1)}, bf16[64,3072]{1,0:T(8,128)(2,1)S(1)}, u32[]{:S(2)}, u32[]{:S(2)}) %collective-permute-start.4) | collective-permute-done | bytes 393248 | tf_op jit(solution)/shard_map/ppermute | solution.py:74
  25.6 2.5 %collective-permute-start.5 = (bf16[256,2048]{1,0:T(8,128)(2,1)S(1)}, bf16[256,2048]{1,0:T(8,128)(2,1)S(1)}, u32[]{:S(2)}, u32[]{:S(2)}) collective-permute-start(bf16[256,2048]{1,0:T(8,128)(2,1)S(1)} %get-tuple-element.66.p0), channel_id=1, source_target_pairs={{0,24},{1,7},{2,26},{3,1},{4,28},{5,3},{6,30},{7,5},{8,0},{9,15},{... | collective-permute-start | bytes 3145736 | tf_op jit(solution)/shard_map/ppermute | solution.py:74
  29.2 2.4 %fusion = f32[1024]{0:T(1024)S(1)} fusion(bf16[512,1024]{1,0:T(8,128)(2,1)S(1)} %copy-done.14, bf16[512,1024]{1,0:T(8,128)(2,1)} %collective-permute-done, pred[]{:T(512)S(6)} %eq.14), kind=kLoop, calls=%fused_computation.2 | loop fusion | flops 12581888 | bytes 2101249 | tf_op jit(solution)/shard_map/reduce_sum | solution.py:700
  31.6 2.3 %multiply_convert_fusion.cot = bf16[1024,1024]{1,0:T(8,128)(2,1)S(1)} fusion(bf16[512,1024]{1,0:T(8,128)(2,1)} %collective-permute-done.8, bf16[512,1024]{1,0:T(8,128)(2,1)S(1)} %copy-done.13, f32[1024]{0:T(1024)S(1)} %bitcast.22, pred[]{:T(512)S(6)} %eq.14), kind=kLoop, calls=%fused_computation.3 | loop fusion | flops 12582912 | bytes 4198401 | tf_op jit(solution)/shard_map/convert_element_type | solution.py:704
  33.9 3.7 %convert_multiply_fusion = (f32[1024,1024]{1,0:T(8,128)}, bf16[1024,1024]{1,0:T(8,128)(2,1)S(1)}) fusion(f32[1024]{0:T(1024)S(1)} %add_rsqrt_fusion, bf16[512,1024]{1,0:T(8,128)(2,1)S(1)} %copy-done.14, bf16[512,1024]{1,0:T(8,128)(2,1)} %collective-permute-done, pred[]{:T(512)S(6)} %eq.14, f32[1024]{0:T(1024)S(1)} %copy-done.7), kind=kLoop, calls=%fused_computation | loop fusion | flops 13631488 | bytes 8396801 | tf_op jit(solution)/shard_map/mul | solution.py:701
  37.6 13.5 %collective-permute-done.5.p1 = bf16[256,2048]{1,0:T(8,128)(2,1)S(1)} collective-permute-done((bf16[256,2048]{1,0:T(8,128)(2,1)S(1)}, bf16[256,2048]{1,0:T(8,128)(2,1)S(1)}, u32[]{:S(2)}, u32[]{:S(2)}) %collective-permute-start.5) | collective-permute-done | bytes 1048608 | tf_op jit(solution)/shard_map/ppermute | solution.py:74
  51.1 3.7 %collective-permute-done.7.p3 = bf16[256,2048]{1,0:T(8,128)(2,1)S(1)} collective-permute-done((bf16[256,2048]{1,0:T(8,128)(2,1)S(1)}, bf16[256,2048]{1,0:T(8,128)(2,1)S(1)}, u32[]{:S(2)}, u32[]{:S(2)}) %collective-permute-start.7) | collective-permute-done | bytes 1048608 | tf_op jit(solution)/shard_map/ppermute | solution.py:74
  55.7 2.1 %collective-permute-start.9 = (bf16[256,1024]{1,0:T(8,128)(2,1)S(1)}, bf16[256,1024]{1,0:T(8,128)(2,1)S(1)}, u32[]{:S(2)}, u32[]{:S(2)}) collective-permute-start(bf16[256,1024]{1,0:T(8,128)(2,1)S(1)} %get-tuple-element.72.p0), channel_id=1, source_target_pairs={{0,24},{1,7},{2,26},{3,1},{4,28},{5,3},{6,30},{7,5},{8,0},{9,15},{... | collective-permute-start | bytes 1572872 | tf_op jit(solution)/shard_map/ppermute | solution.py:74
  57.9 10.5 %project.1 = (bf16[1024,2048]{1,0:T(8,128)(2,1)S(1)}, bf16[1024,512]{1,0:T(8,128)(2,1)S(1)}, bf16[1024,2048]{1,0:T(8,128)(2,1)S(1)}) custom-call(s32[4]{0:T(128)S(1)} %pad_add_fusion.ids, bf16[1024,1024]{1,0:T(8,128)(2,1)S(1)} %get-tuple-element.65.normed.x_in, f32[1024,128]{1,0:T(8,128)S(1)} %get-tuple-element.121.cos, ...), custom_call_target="tpu_custom_call" | custom-call | flops 1024 | bytes 1024 | tf_op jit(solution)/shard_map/project/pallas_call | solution.py:172
  68.4 2.0 %copy-done.2 = bf16[1024,2048]{1,0:T(8,128)(2,1)} copy-done((bf16[1024,2048]{1,0:T(8,128)(2,1)}, bf16[1024,2048]{1,0:T(8,128)(2,1)S(1)}, u32[]{:S(2)}) %copy-start.2) | copy-done | bytes 4194328
  70.4 7.3 %attend.1 = (bf16[1024,512]{1,0:T(8,128)(2,1)S(1)}, bf16[1024,512]{1,0:T(8,128)(2,1)S(1)}, f32[8,2,512]{2,1,0:T(2,128)S(1)}) custom-call(s32[4]{0:T(128)S(1)} %pad_add_fusion.ids, bf16[1024,2048]{1,0:T(8,128)(2,1)S(1)} %get-tuple-element.70.qkv, s32[2,1,512]{2,1,0:T(1,128)S(1)} %broadcast_in_dim.82.start), custom_call_target="tpu_custom_call" | custom-call | flops 1024 | bytes 1024 | tf_op jit(solution)/shard_map/attend/pallas_call | solution.py:269
  77.7 3.5 %collective-permute-start.13 = (bf16[1024,512]{1,0:T(8,128)(2,1)S(1)}, bf16[1024,512]{1,0:T(8,128)(2,1)S(1)}, u32[]{:S(2)}, u32[]{:S(2)}) collective-permute-start(bf16[1024,512]{1,0:T(8,128)(2,1)S(1)} %get-tuple-element.85), channel_id=1, source_target_pairs={{0,1},{1,0},{2,3},{3,2},{4,5},{5,4},{6,7},{7,6},{8,9},{9,8},{10,11... | collective-permute-start | bytes 3145736 | tf_op jit(solution)/shard_map/ppermute | solution.py:40
  81.3 3.3 %to_mixed.1 = (bf16[1024,512]{1,0:T(8,128)(2,1)S(1)}, bf16[1024,512]{1,0:T(8,128)(2,1)S(1)}) custom-call(s32[4]{0:T(128)S(1)} %pad_add_fusion.ids, bf16[1024,1024]{1,0:T(8,128)(2,1)S(1)} %multiply_convert_fusion.cot, bf16[256,1024]{1,0:T(8,128)(2,1)S(1)} %get-tuple-element.72.p0, bf16[256,1024]{1,0:T(8,128)(2,1)S(1)} %collective-permute-done.9.p1, ...), custom_call_target="tpu_custom_call" | custom-call | flops 1024 | bytes 1024 | tf_op jit(solution)/shard_map/to_mixed/pallas_call | solution.py:521
  84.7 3.7 %output_pieces.1 = (bf16[256,1024]{1,0:T(8,128)(2,1)S(1)}, bf16[256,1024]{1,0:T(8,128)(2,1)S(1)}, bf16[256,1024]{1,0:T(8,128)(2,1)S(1)}, bf16[256,1024]{1,0:T(8,128)(2,1)S(1)}) custom-call(s32[4]{0:T(128)S(1)} %pad_add_fusion.ids, bf16[1024,512]{1,0:T(8,128)(2,1)S(1)} %get-tuple-element.84.keep, bf16[1024,512]{1,0:T(8,128)(2,1)S(1)} %collective-permute-done.13.got, ...), custom_call_target="tpu_custom_call" | custom-call | flops 1024 | bytes 1024 | tf_op jit(solution)/shard_map/output_pieces/pallas_call | solution.py:560
  88.6 2.7 %collective-permute-start.15 = (bf16[256,1024]{1,0:T(8,128)(2,1)S(1)}, bf16[256,1024]{1,0:T(8,128)(2,1)S(1)}, u32[]{:S(2)}, u32[]{:S(2)}) collective-permute-start(bf16[256,1024]{1,0:T(8,128)(2,1)S(1)} %get-tuple-element.88), channel_id=1, source_target_pairs={{0,24},{1,7},{2,26},{3,1},{4,28},{5,3},{6,30},{7,5},{8,0},{9,15},{... | collective-permute-start | bytes 1572872 | tf_op jit(solution)/shard_map/ppermute | solution.py:74
  91.3 27.1 %attend_back.1 = (bf16[1024,2048]{1,0:T(8,128)(2,1)}, bf16[256,2176]{1,0:T(8,128)(2,1)S(1)}, bf16[256,2176]{1,0:T(8,128)(2,1)}, bf16[256,2176]{1,0:T(8,128)(2,1)}, bf16[256,2176]{1,0:T(8,128)(2,1)}) custom-call(s32[4]{0:T(128)S(1)} %pad_add_fusion.ids, bf16[1024,2048]{1,0:T(8,128)(2,1)} %copy-done.1, bf16[1024,512]{1,0:T(8,128)(2,1)S(1)} %get-tuple-element.73.dm_a, ...), custom_call_target="tpu_custom_call" | custom-call | flops 1024 | bytes 1024 | tf_op jit(solution)/shard_map/attend_back/pallas_call | solution.py:459
  119.0 2.1 %collective-permute-start.19 = (bf16[256,2176]{1,0:T(8,128)(2,1)}, bf16[256,2176]{1,0:T(8,128)(2,1)S(1)}, u32[]{:S(2)}, u32[]{:S(2)}) collective-permute-start(bf16[256,2176]{1,0:T(8,128)(2,1)} %get-tuple-element.95), channel_id=1, source_target_pairs={{0,24},{1,7},{2,26},{3,1},{4,28},{5,3},{6,30},{7,5},{8,0},{9,15},{... | collective-permute-start | bytes 3342344 | tf_op jit(solution)/shard_map/ppermute | solution.py:74
  122.9 2.2 %copy-done.4 = bf16[1024,2048]{1,0:T(8,128)(2,1)S(1)} copy-done((bf16[1024,2048]{1,0:T(8,128)(2,1)S(1)}, bf16[1024,2048]{1,0:T(8,128)(2,1)}, u32[]{:S(2)}) %copy-start.4) | copy-done | bytes 4194328
  125.1 6.0 %to_normed.1 = (bf16[512,1024]{1,0:T(8,128)(2,1)S(1)}, f32[512,1024]{1,0:T(8,128)S(1)}) custom-call(s32[4]{0:T(128)S(1)} %pad_add_fusion.ids, bf16[1024,2048]{1,0:T(8,128)(2,1)S(1)} %copy-done.4, bf16[1024,2048]{1,0:T(8,128)(2,1)S(1)} %copy-done.3), custom_call_target="tpu_custom_call" | custom-call | flops 1024 | bytes 1024 | tf_op jit(solution)/shard_map/to_normed/pallas_call | solution.py:590
  131.0 2.2 %collective-permute-start.17 = (bf16[512,1024]{1,0:T(8,128)(2,1)S(1)}, bf16[512,1024]{1,0:T(8,128)(2,1)S(1)}, u32[]{:S(2)}, u32[]{:S(2)}) collective-permute-start(bf16[512,1024]{1,0:T(8,128)(2,1)S(1)} %get-tuple-element.92), channel_id=1, source_target_pairs={{0,1},{1,0},{2,3},{3,2},{4,5},{5,4},{6,7},{7,6},{8,9},{9,8},{10,11... | collective-permute-start | bytes 3145736 | tf_op jit(solution)/shard_map/ppermute | solution.py:40
  134.5 11.3 %collective-permute-done.19.refs_2_ = bf16[256,2176]{1,0:T(8,128)(2,1)S(1)} collective-permute-done((bf16[256,2176]{1,0:T(8,128)(2,1)}, bf16[256,2176]{1,0:T(8,128)(2,1)S(1)}, u32[]{:S(2)}, u32[]{:S(2)}) %collective-permute-start.19) | collective-permute-done | bytes 1114144 | tf_op jit(solution)/shard_map/ppermute | solution.py:74
  148.2 2.7 %collective-permute-start.22 = (bf16[64,3200]{1,0:T(8,128)(2,1)S(1)}, bf16[64,3200]{1,0:T(8,128)(2,1)S(1)}, u32[]{:S(2)}, u32[]{:S(2)}) collective-permute-start(bf16[64,3200]{1,0:T(8,128)(2,1)S(1)} %get-tuple-element.103), channel_id=1, source_target_pairs={{0,6},{1,25},{2,0},{3,27},{4,2},{5,29},{6,4},{7,31},{8,14},{9,1},{... | collective-permute-start | bytes 1228808 | tf_op jit(solution)/shard_map/ppermute | solution.py:74
  151.6 9.3 %collective-permute-done.21.b = bf16[64,3200]{1,0:T(8,128)(2,1)S(1)} collective-permute-done((bf16[64,3200]{1,0:T(8,128)(2,1)S(1)}, bf16[64,3200]{1,0:T(8,128)(2,1)S(1)}, u32[]{:S(2)}, u32[]{:S(2)}) %collective-permute-start.21) | collective-permute-done | bytes 409632 | tf_op jit(solution)/shard_map/ppermute | solution.py:74
  161.7 3.3 %collective-permute-start.24 = (bf16[32,2176]{1,0:T(8,128)(2,1)S(1)}, bf16[32,2176]{1,0:T(8,128)(2,1)S(1)}, u32[]{:S(2)}, u32[]{:S(2)}) collective-permute-start(bf16[32,2176]{1,0:T(8,128)(2,1)S(1)} %get-tuple-element.106), channel_id=1, source_target_pairs={{0,1},{1,0},{2,3},{3,2},{4,5},{5,4},{6,7},{7,6},{8,9},{9,8},{10,11... | collective-permute-start | bytes 417800 | tf_op jit(solution)/shard_map/ppermute | solution.py:40
  166.0 2.8 %collective-permute-start.25 = (bf16[32,6400]{1,0:T(8,128)(2,1)S(1)}, bf16[32,6400]{1,0:T(8,128)(2,1)S(1)}, u32[]{:S(2)}, u32[]{:S(2)}) collective-permute-start(bf16[32,6400]{1,0:T(8,128)(2,1)S(1)} %constant_dynamic-update-slice_fusion.a), channel_id=1, source_target_pairs={{0,64},{32,96},{64,0},{96,32},{1,65},{33,97},{65,1},{97,33},{2,66}... | collective-permute-start | bytes 1228808 | tf_op jit(solution)/shard_map/ppermute | solution.py:36
  169.1 2.4 %collective-permute-start.27 = (bf16[32,6400]{1,0:T(8,128)(2,1)S(1)}, bf16[32,6400]{1,0:T(8,128)(2,1)S(1)}, u32[]{:S(2)}, u32[]{:S(2)}) collective-permute-start(bf16[32,6400]{1,0:T(8,128)(2,1)S(1)} %constant_dynamic-update-slice_fusion.a), channel_id=1, source_target_pairs={{0,96},{32,0},{64,32},{96,64},{1,97},{33,1},{65,33},{97,65},{2,98}... | collective-permute-start | bytes 1228808 | tf_op jit(solution)/shard_map/ppermute | solution.py:36
  171.5 1.8 add_convert_fusion
  173.2 5.1 %collective-permute-done.25.b = bf16[32,6400]{1,0:T(8,128)(2,1)S(1)} collective-permute-done((bf16[32,6400]{1,0:T(8,128)(2,1)S(1)}, bf16[32,6400]{1,0:T(8,128)(2,1)S(1)}, u32[]{:S(2)}, u32[]{:S(2)}) %collective-permute-start.25) | collective-permute-done | bytes 409632 | tf_op jit(solution)/shard_map/ppermute | solution.py:36
  178.3 9.4 %collective-permute-done.26.c = bf16[32,6400]{1,0:T(8,128)(2,1)S(1)} collective-permute-done((bf16[32,6400]{1,0:T(8,128)(2,1)S(1)}, bf16[32,6400]{1,0:T(8,128)(2,1)S(1)}, u32[]{:S(2)}, u32[]{:S(2)}) %collective-permute-start.26) | collective-permute-done | bytes 409632 | tf_op jit(solution)/shard_map/ppermute | solution.py:36
  (97 shorter events, 24.5 us)
Async XLA Ops:
  4.7 2.6 %collective-permute-start.1 = (bf16[48,2048]{1,0:T(8,128)(2,1)S(1)}, bf16[48,2048]{1,0:T(8,128)(2,1)S(1)}, u32[]{:S(2)}, u32[]{:S(2)}) collective-permute-start(bf16[48,2048]{1,0:T(8,128)(2,1)S(1)} %get-tuple-element.62), channel_id=1, source_target_pairs={{0,1},{1,0},{2,3},{3,2},{4,5},{5,4},{6,7},{7,6},{8,9},{9,8},{10,11... | collective-permute-start | bytes 589832 | tf_op jit(solution)/shard_map/ppermute | solution.py:40
  6.2 25.4 %collective-permute-start.8 = (bf16[512,1024]{1,0:T(8,128)(2,1)}, bf16[512,1024]{1,0:T(8,128)(2,1)}, u32[]{:S(2)}, u32[]{:S(2)}) collective-permute-start(bf16[512,1024]{1,0:T(8,128)(2,1)} %param.13), channel_id=1, source_target_pairs={{0,1},{1,0},{2,3},{3,2},{4,5},{5,4},{6,7},{7,6},{8,9},{9,8},{10,11... | collective-permute-start | bytes 3145736 | tf_op jit(solution)/shard_map/ppermute | solution.py:40
  6.3 22.9 %collective-permute-start = (bf16[512,1024]{1,0:T(8,128)(2,1)}, bf16[512,1024]{1,0:T(8,128)(2,1)}, u32[]{:S(2)}, u32[]{:S(2)}) collective-permute-start(bf16[512,1024]{1,0:T(8,128)(2,1)} %param.12), channel_id=1, source_target_pairs={{0,1},{1,0},{2,3},{3,2},{4,5},{5,4},{6,7},{7,6},{8,9},{9,8},{10,11... | collective-permute-start | bytes 3145736 | tf_op jit(solution)/shard_map/ppermute | solution.py:40
  8.7 12.8 %collective-permute-start.2 = (bf16[64,3072]{1,0:T(8,128)(2,1)S(1)}, bf16[64,3072]{1,0:T(8,128)(2,1)S(1)}, u32[]{:S(2)}, u32[]{:S(2)}) collective-permute-start(bf16[64,3072]{1,0:T(8,128)(2,1)S(1)} %join.1.p0), channel_id=1, source_target_pairs={{0,6},{1,25},{2,0},{3,27},{4,2},{5,29},{6,4},{7,31},{8,14},{9,1},{... | collective-permute-start | bytes 1179656 | tf_op jit(solution)/shard_map/ppermute | solution.py:74
  12.6 8.9 %collective-permute-start.3 = (bf16[64,3072]{1,0:T(8,128)(2,1)S(1)}, bf16[64,3072]{1,0:T(8,128)(2,1)S(1)}, u32[]{:S(2)}, u32[]{:S(2)}) collective-permute-start(bf16[64,3072]{1,0:T(8,128)(2,1)S(1)} %join.1.p0), channel_id=1, source_target_pairs={{0,4},{1,17},{2,6},{3,19},{4,0},{5,21},{6,2},{7,23},{8,12},{9,25},... | collective-permute-start | bytes 1179656 | tf_op jit(solution)/shard_map/ppermute | solution.py:74
  12.6 12.3 %collective-permute-start.4 = (bf16[64,3072]{1,0:T(8,128)(2,1)S(1)}, bf16[64,3072]{1,0:T(8,128)(2,1)S(1)}, u32[]{:S(2)}, u32[]{:S(2)}) collective-permute-start(bf16[64,3072]{1,0:T(8,128)(2,1)S(1)} %join.1.p0), channel_id=1, source_target_pairs={{0,2},{1,9},{2,4},{3,11},{4,6},{5,13},{6,0},{7,15},{8,10},{9,17},{... | collective-permute-start | bytes 1179656 | tf_op jit(solution)/shard_map/ppermute | solution.py:74
  25.6 25.5 %collective-permute-start.5 = (bf16[256,2048]{1,0:T(8,128)(2,1)S(1)}, bf16[256,2048]{1,0:T(8,128)(2,1)S(1)}, u32[]{:S(2)}, u32[]{:S(2)}) collective-permute-start(bf16[256,2048]{1,0:T(8,128)(2,1)S(1)} %get-tuple-element.66.p0), channel_id=1, source_target_pairs={{0,24},{1,7},{2,26},{3,1},{4,28},{5,3},{6,30},{7,5},{8,0},{9,15},{... | collective-permute-start | bytes 3145736 | tf_op jit(solution)/shard_map/ppermute | solution.py:74
  28.1 23.0 %collective-permute-start.6 = (bf16[256,2048]{1,0:T(8,128)(2,1)S(1)}, bf16[256,2048]{1,0:T(8,128)(2,1)S(1)}, u32[]{:S(2)}, u32[]{:S(2)}) collective-permute-start(bf16[256,2048]{1,0:T(8,128)(2,1)S(1)} %get-tuple-element.66.p0), channel_id=1, source_target_pairs={{0,16},{1,5},{2,18},{3,7},{4,20},{5,1},{6,22},{7,3},{8,24},{9,13},... | collective-permute-start | bytes 3145736 | tf_op jit(solution)/shard_map/ppermute | solution.py:74
  28.5 26.3 %collective-permute-start.7 = (bf16[256,2048]{1,0:T(8,128)(2,1)S(1)}, bf16[256,2048]{1,0:T(8,128)(2,1)S(1)}, u32[]{:S(2)}, u32[]{:S(2)}) collective-permute-start(bf16[256,2048]{1,0:T(8,128)(2,1)S(1)} %get-tuple-element.66.p0), channel_id=1, source_target_pairs={{0,8},{1,3},{2,10},{3,5},{4,12},{5,7},{6,14},{7,1},{8,16},{9,11},{... | collective-permute-start | bytes 3145736 | tf_op jit(solution)/shard_map/ppermute | solution.py:74
  33.9 24.0 %copy-start.10 = (f32[128]{0:T(128)S(1)}, f32[128]{0:T(128)}, u32[]{:S(2)}) copy-start(f32[128]{0:T(128)} %param.18) | copy-start | bytes 1540
  33.9 24.0 %copy-start.11 = (f32[128]{0:T(128)S(1)}, f32[128]{0:T(128)}, u32[]{:S(2)}) copy-start(f32[128]{0:T(128)} %param.19) | copy-start | bytes 1540
  37.6 30.8 %copy-start = (bf16[1024,1024]{1,0:T(8,128)(2,1)}, bf16[1024,1024]{1,0:T(8,128)(2,1)S(1)}, u32[]{:S(2)}) copy-start(bf16[1024,1024]{1,0:T(8,128)(2,1)S(1)} %get-tuple-element.65.normed.x_in) | copy-start | bytes 6291460
  54.8 26.4 %collective-permute-start.10 = (bf16[256,1024]{1,0:T(8,128)(2,1)S(1)}, bf16[256,1024]{1,0:T(8,128)(2,1)S(1)}, u32[]{:S(2)}, u32[]{:S(2)}) collective-permute-start(bf16[256,1024]{1,0:T(8,128)(2,1)S(1)} %get-tuple-element.72.p0), channel_id=1, source_target_pairs={{0,16},{1,5},{2,18},{3,7},{4,20},{5,1},{6,22},{7,3},{8,24},{9,13},... | collective-permute-start | bytes 1572872 | tf_op jit(solution)/shard_map/ppermute | solution.py:74
  55.2 26.1 %collective-permute-start.11 = (bf16[256,1024]{1,0:T(8,128)(2,1)S(1)}, bf16[256,1024]{1,0:T(8,128)(2,1)S(1)}, u32[]{:S(2)}, u32[]{:S(2)}) collective-permute-start(bf16[256,1024]{1,0:T(8,128)(2,1)S(1)} %get-tuple-element.72.p0), channel_id=1, source_target_pairs={{0,8},{1,3},{2,10},{3,5},{4,12},{5,7},{6,14},{7,1},{8,16},{9,11},{... | collective-permute-start | bytes 1572872 | tf_op jit(solution)/shard_map/ppermute | solution.py:74
  55.7 25.6 %collective-permute-start.9 = (bf16[256,1024]{1,0:T(8,128)(2,1)S(1)}, bf16[256,1024]{1,0:T(8,128)(2,1)S(1)}, u32[]{:S(2)}, u32[]{:S(2)}) collective-permute-start(bf16[256,1024]{1,0:T(8,128)(2,1)S(1)} %get-tuple-element.72.p0), channel_id=1, source_target_pairs={{0,24},{1,7},{2,26},{3,1},{4,28},{5,3},{6,30},{7,5},{8,0},{9,15},{... | collective-permute-start | bytes 1572872 | tf_op jit(solution)/shard_map/ppermute | solution.py:74
  77.7 7.0 %collective-permute-start.13 = (bf16[1024,512]{1,0:T(8,128)(2,1)S(1)}, bf16[1024,512]{1,0:T(8,128)(2,1)S(1)}, u32[]{:S(2)}, u32[]{:S(2)}) collective-permute-start(bf16[1024,512]{1,0:T(8,128)(2,1)S(1)} %get-tuple-element.85), channel_id=1, source_target_pairs={{0,1},{1,0},{2,3},{3,2},{4,5},{5,4},{6,7},{7,6},{8,9},{9,8},{10,11... | collective-permute-start | bytes 3145736 | tf_op jit(solution)/shard_map/ppermute | solution.py:40
  84.6 6.6 %collective-permute-start.12 = (bf16[1024,512]{1,0:T(8,128)(2,1)S(1)}, bf16[1024,512]{1,0:T(8,128)(2,1)S(1)}, u32[]{:S(2)}, u32[]{:S(2)}) collective-permute-start(bf16[1024,512]{1,0:T(8,128)(2,1)S(1)} %get-tuple-element.74), channel_id=1, source_target_pairs={{0,1},{1,0},{2,3},{3,2},{4,5},{5,4},{6,7},{7,6},{8,9},{9,8},{10,11... | collective-permute-start | bytes 3145736 | tf_op jit(solution)/shard_map/ppermute | solution.py:40
  88.5 29.9 %collective-permute-start.14 = (bf16[256,1024]{1,0:T(8,128)(2,1)S(1)}, bf16[256,1024]{1,0:T(8,128)(2,1)S(1)}, u32[]{:S(2)}, u32[]{:S(2)}) collective-permute-start(bf16[256,1024]{1,0:T(8,128)(2,1)S(1)} %get-tuple-element.87), channel_id=1, source_target_pairs={{0,8},{1,3},{2,10},{3,5},{4,12},{5,7},{6,14},{7,1},{8,16},{9,11},{... | collective-permute-start | bytes 1572872 | tf_op jit(solution)/shard_map/ppermute | solution.py:74
  88.6 29.8 %collective-permute-start.15 = (bf16[256,1024]{1,0:T(8,128)(2,1)S(1)}, bf16[256,1024]{1,0:T(8,128)(2,1)S(1)}, u32[]{:S(2)}, u32[]{:S(2)}) collective-permute-start(bf16[256,1024]{1,0:T(8,128)(2,1)S(1)} %get-tuple-element.88), channel_id=1, source_target_pairs={{0,24},{1,7},{2,26},{3,1},{4,28},{5,3},{6,30},{7,5},{8,0},{9,15},{... | collective-permute-start | bytes 1572872 | tf_op jit(solution)/shard_map/ppermute | solution.py:74
  91.2 27.1 %collective-permute-start.16 = (bf16[256,1024]{1,0:T(8,128)(2,1)S(1)}, bf16[256,1024]{1,0:T(8,128)(2,1)S(1)}, u32[]{:S(2)}, u32[]{:S(2)}) collective-permute-start(bf16[256,1024]{1,0:T(8,128)(2,1)S(1)} %get-tuple-element.89), channel_id=1, source_target_pairs={{0,16},{1,5},{2,18},{3,7},{4,20},{5,1},{6,22},{7,3},{8,24},{9,13},... | collective-permute-start | bytes 1572872 | tf_op jit(solution)/shard_map/ppermute | solution.py:74
  91.3 31.6 %copy-start.3 = (bf16[1024,2048]{1,0:T(8,128)(2,1)S(1)}, bf16[1024,2048]{1,0:T(8,128)(2,1)}, u32[]{:S(2)}) copy-start(bf16[1024,2048]{1,0:T(8,128)(2,1)} %copy-done.2) | copy-start | bytes 12582916
  118.4 16.1 %collective-permute-start.18 = (bf16[256,2176]{1,0:T(8,128)(2,1)}, bf16[256,2176]{1,0:T(8,128)(2,1)S(1)}, u32[]{:S(2)}, u32[]{:S(2)}) collective-permute-start(bf16[256,2176]{1,0:T(8,128)(2,1)} %get-tuple-element.94), channel_id=1, source_target_pairs={{0,8},{1,3},{2,10},{3,5},{4,12},{5,7},{6,14},{7,1},{8,16},{9,11},{... | collective-permute-start | bytes 3342344 | tf_op jit(solution)/shard_map/ppermute | solution.py:74
  119.0 26.9 %collective-permute-start.19 = (bf16[256,2176]{1,0:T(8,128)(2,1)}, bf16[256,2176]{1,0:T(8,128)(2,1)S(1)}, u32[]{:S(2)}, u32[]{:S(2)}) collective-permute-start(bf16[256,2176]{1,0:T(8,128)(2,1)} %get-tuple-element.95), channel_id=1, source_target_pairs={{0,24},{1,7},{2,26},{3,1},{4,28},{5,3},{6,30},{7,5},{8,0},{9,15},{... | collective-permute-start | bytes 3342344 | tf_op jit(solution)/shard_map/ppermute | solution.py:74
  121.1 25.6 %collective-permute-start.20 = (bf16[256,2176]{1,0:T(8,128)(2,1)}, bf16[256,2176]{1,0:T(8,128)(2,1)S(1)}, u32[]{:S(2)}, u32[]{:S(2)}) collective-permute-start(bf16[256,2176]{1,0:T(8,128)(2,1)} %get-tuple-element.96), channel_id=1, source_target_pairs={{0,16},{1,5},{2,18},{3,7},{4,20},{5,1},{6,22},{7,3},{8,24},{9,13},... | collective-permute-start | bytes 3342344 | tf_op jit(solution)/shard_map/ppermute | solution.py:74
  131.0 20.1 %collective-permute-start.17 = (bf16[512,1024]{1,0:T(8,128)(2,1)S(1)}, bf16[512,1024]{1,0:T(8,128)(2,1)S(1)}, u32[]{:S(2)}, u32[]{:S(2)}) collective-permute-start(bf16[512,1024]{1,0:T(8,128)(2,1)S(1)} %get-tuple-element.92), channel_id=1, source_target_pairs={{0,1},{1,0},{2,3},{3,2},{4,5},{5,4},{6,7},{7,6},{8,9},{9,8},{10,11... | collective-permute-start | bytes 3145736 | tf_op jit(solution)/shard_map/ppermute | solution.py:40
  148.1 12.8 %collective-permute-start.21 = (bf16[64,3200]{1,0:T(8,128)(2,1)S(1)}, bf16[64,3200]{1,0:T(8,128)(2,1)S(1)}, u32[]{:S(2)}, u32[]{:S(2)}) collective-permute-start(bf16[64,3200]{1,0:T(8,128)(2,1)S(1)} %get-tuple-element.102), channel_id=1, source_target_pairs={{0,2},{1,9},{2,4},{3,11},{4,6},{5,13},{6,0},{7,15},{8,10},{9,17},{... | collective-permute-start | bytes 1228808 | tf_op jit(solution)/shard_map/ppermute | solution.py:74
  148.2 12.7 %collective-permute-start.22 = (bf16[64,3200]{1,0:T(8,128)(2,1)S(1)}, bf16[64,3200]{1,0:T(8,128)(2,1)S(1)}, u32[]{:S(2)}, u32[]{:S(2)}) collective-permute-start(bf16[64,3200]{1,0:T(8,128)(2,1)S(1)} %get-tuple-element.103), channel_id=1, source_target_pairs={{0,6},{1,25},{2,0},{3,27},{4,2},{5,29},{6,4},{7,31},{8,14},{9,1},{... | collective-permute-start | bytes 1228808 | tf_op jit(solution)/shard_map/ppermute | solution.py:74
  150.9 10.0 %collective-permute-start.23 = (bf16[64,3200]{1,0:T(8,128)(2,1)S(1)}, bf16[64,3200]{1,0:T(8,128)(2,1)S(1)}, u32[]{:S(2)}, u32[]{:S(2)}) collective-permute-start(bf16[64,3200]{1,0:T(8,128)(2,1)S(1)} %get-tuple-element.104), channel_id=1, source_target_pairs={{0,4},{1,17},{2,6},{3,19},{4,0},{5,21},{6,2},{7,23},{8,12},{9,25},... | collective-permute-start | bytes 1228808 | tf_op jit(solution)/shard_map/ppermute | solution.py:74
  161.7 4.3 %collective-permute-start.24 = (bf16[32,2176]{1,0:T(8,128)(2,1)S(1)}, bf16[32,2176]{1,0:T(8,128)(2,1)S(1)}, u32[]{:S(2)}, u32[]{:S(2)}) collective-permute-start(bf16[32,2176]{1,0:T(8,128)(2,1)S(1)} %get-tuple-element.106), channel_id=1, source_target_pairs={{0,1},{1,0},{2,3},{3,2},{4,5},{5,4},{6,7},{7,6},{8,9},{9,8},{10,11... | collective-permute-start | bytes 417800 | tf_op jit(solution)/shard_map/ppermute | solution.py:40
  166.0 12.3 %collective-permute-start.25 = (bf16[32,6400]{1,0:T(8,128)(2,1)S(1)}, bf16[32,6400]{1,0:T(8,128)(2,1)S(1)}, u32[]{:S(2)}, u32[]{:S(2)}) collective-permute-start(bf16[32,6400]{1,0:T(8,128)(2,1)S(1)} %constant_dynamic-update-slice_fusion.a), channel_id=1, source_target_pairs={{0,64},{32,96},{64,0},{96,32},{1,65},{33,97},{65,1},{97,33},{2,66}... | collective-permute-start | bytes 1228808 | tf_op jit(solution)/shard_map/ppermute | solution.py:36
  168.8 18.9 %collective-permute-start.26 = (bf16[32,6400]{1,0:T(8,128)(2,1)S(1)}, bf16[32,6400]{1,0:T(8,128)(2,1)S(1)}, u32[]{:S(2)}, u32[]{:S(2)}) collective-permute-start(bf16[32,6400]{1,0:T(8,128)(2,1)S(1)} %constant_dynamic-update-slice_fusion.a), channel_id=1, source_target_pairs={{0,32},{32,64},{64,96},{96,0},{1,33},{33,65},{65,97},{97,1},{2,34}... | collective-permute-start | bytes 1228808 | tf_op jit(solution)/shard_map/ppermute | solution.py:36
  169.1 18.6 %collective-permute-start.27 = (bf16[32,6400]{1,0:T(8,128)(2,1)S(1)}, bf16[32,6400]{1,0:T(8,128)(2,1)S(1)}, u32[]{:S(2)}, u32[]{:S(2)}) collective-permute-start(bf16[32,6400]{1,0:T(8,128)(2,1)S(1)} %constant_dynamic-update-slice_fusion.a), channel_id=1, source_target_pairs={{0,96},{32,0},{64,32},{96,64},{1,97},{33,1},{65,33},{97,65},{2,98}... | collective-permute-start | bytes 1228808 | tf_op jit(solution)/shard_map/ppermute | solution.py:36
  (11 other events, 60.6 us)
